TPU v7x, 512 devices: a whole 4x4x16 slice. The times are simulated.
512 devices in a mesh: ty: 32 (over y, x, core), tx: 16 (over z).
Axes of the slice: x: 4, y: 4, z: 16, core: 2. Of those that a mesh axis runs over, the one named last changes fastest.
Arguments:
- features: bfloat16 [9, 1024, 4096], P(None, 'ty', 'tx'), may hold values from -6 to 6
- enc_conv0: bfloat16 [3, 3, 32, 9], replicated, may hold values from -1 to 1
- enc_conv1: bfloat16 [3, 3, 32, 32], replicated, may hold values from -0.5 to 0.5
- enc_conv2: bfloat16 [3, 3, 48, 32], replicated, may hold values from -0.5 to 0.5
- enc_conv3: bfloat16 [3, 3, 64, 48], replicated, may hold values from -0.4375 to 0.4375
- enc_conv4: bfloat16 [3, 3, 80, 64], replicated, may hold values from -0.375 to 0.375
- enc_conv5a: bfloat16 [3, 3, 96, 80], replicated, may hold values from -0.3125 to 0.3125
- enc_conv5b: bfloat16 [3, 3, 96, 96], replicated, may hold values from -0.3125 to 0.3125
- dec_conv4a: bfloat16 [3, 3, 112, 160], replicated, may hold values from -0.21875 to 0.21875
- dec_conv4b: bfloat16 [3, 3, 112, 112], replicated, may hold values from -0.25 to 0.25
- dec_conv3a: bfloat16 [3, 3, 96, 160], replicated, may hold values from -0.21875 to 0.21875
- dec_conv3b: bfloat16 [3, 3, 96, 96], replicated, may hold values from -0.3125 to 0.3125
- dec_conv2a: bfloat16 [3, 3, 64, 128], replicated, may hold values from -0.25 to 0.25
- dec_conv2b: bfloat16 [3, 3, 64, 64], replicated, may hold values from -0.375 to 0.375
- dec_conv1a: bfloat16 [3, 3, 64, 73], replicated, may hold values from -0.3125 to 0.3125
- dec_conv1b: bfloat16 [3, 3, 32, 64], replicated, may hold values from -0.375 to 0.375
- dec_conv0: bfloat16 [3, 3, 3, 32], replicated, may hold values from -0.375 to 0.375
- biases: float32 [1091], replicated, may hold values from -1 to 1
Outputs:
- denoised: bfloat16 [3, 1024, 4096], P(None, 'ty', 'tx')
All inputs are finite; a program needn't handle non-finite values.
Results may differ from a plain program's by a relative error of at most 0.038.
Values may be sent and summed in bfloat16 or wider, within the bound.
A program may use at most 64 MiB of HBM per device.

v0:
```python
import jax
import jax.numpy as jnp
from jax import lax
from jax.sharding import PartitionSpec as P


def with_halo(array, sides, width):
    for axis, dim in sides:
        size, length = (lax.axis_size(axis), array.shape[dim])
        up = [(i, (i + 1) % size) for i in range(size - 1)]
        down = [(j, i) for i, j in up]
        last = lax.slice_in_dim(array, length - width, length, axis=dim)
        initial = lax.slice_in_dim(array, 0, width, axis=dim)
        before = lax.ppermute(last, axis, up)
        after = lax.ppermute(initial, axis, down)
        array = jnp.concatenate([before, array, after], axis=dim)
    return array


def split_biases(biases, weights):
    pieces = []
    offset = 0
    for weight in weights:
        count = weight.shape[2]
        pieces.append(biases[offset : offset + count])
        offset = offset + count
    return pieces


def convolve_tile(padded, weight, bias_vec, active):
    height = padded.shape[1] - 2
    columns = padded.shape[2] - 2
    summed = jnp.zeros((weight.shape[2], height, columns), jnp.float32)
    for row_off in range(3):
        for col_off in range(3):
            summed = summed + jnp.einsum(
                "oc,chw->ohw",
                weight[row_off, col_off],
                padded[:, row_off : row_off + height, col_off : col_off + columns],
                preferred_element_type=jnp.float32,
            )
    summed = summed + bias_vec[:, None, None]
    if active:
        summed = jax.nn.relu(summed)
    return summed.astype(jnp.bfloat16)


def max_pool(field):
    channels, height, columns = field.shape
    return field.reshape(channels, height // 2, 2, columns // 2, 2).max(axis=(2, 4))


def upsample(field):
    channels, height, columns = field.shape
    return jnp.broadcast_to(field[:, :, None, :, None], (channels, height, 2, columns, 2)).reshape(
        channels, 2 * height, 2 * columns
    )


def fine_border(field):
    return with_halo(field, (("ty", 1), ("tx", 2)), 1)


def coarse_border(field):
    return with_halo(field, (("ty", 1), ("tx", 2)), 1)


def body(
    features,
    enc_conv0,
    enc_conv1,
    enc_conv2,
    enc_conv3,
    enc_conv4,
    enc_conv5a,
    enc_conv5b,
    dec_conv4a,
    dec_conv4b,
    dec_conv3a,
    dec_conv3b,
    dec_conv2a,
    dec_conv2b,
    dec_conv1a,
    dec_conv1b,
    dec_conv0,
    biases,
):
    weights = [
        enc_conv0,
        enc_conv1,
        enc_conv2,
        enc_conv3,
        enc_conv4,
        enc_conv5a,
        enc_conv5b,
        dec_conv4a,
        dec_conv4b,
        dec_conv3a,
        dec_conv3b,
        dec_conv2a,
        dec_conv2b,
        dec_conv1a,
        dec_conv1b,
        dec_conv0,
    ]
    shifts = split_biases(biases, weights)

    def layer(number, padded):
        return convolve_tile(padded, weights[number], shifts[number], number < 15)

    def two_layers(first, field):
        narrow = fine_border(field)
        return (layer(first + 1, fine_border(layer(first, narrow))), narrow)

    full_res, input_border = two_layers(0, features)
    pooled_one = max_pool(full_res)
    half_res = layer(2, fine_border(pooled_one))
    pooled_two = max_pool(half_res)
    quarter_res = layer(3, fine_border(pooled_two))
    pooled_three = max_pool(quarter_res)
    eighth_res = layer(4, coarse_border(pooled_three))
    bottom = layer(6, coarse_border(layer(5, coarse_border(max_pool(eighth_res)))))
    joined = jnp.concatenate([upsample(bottom), pooled_three], 0)
    rise_four = layer(8, coarse_border(layer(7, coarse_border(joined))))
    lifted_four = upsample(rise_four)
    rise_three, unused_three = two_layers(9, jnp.concatenate([lifted_four, pooled_two], 0))
    rise_two, unused_two = two_layers(11, jnp.concatenate([upsample(rise_three), pooled_one], 0))
    merged = fine_border(jnp.concatenate([upsample(rise_two), features], 0))
    first_dec = layer(13, merged)
    denoised, unused_last = two_layers(14, first_dec)
    return denoised


def solution(mesh):
    return jax.shard_map(
        body,
        mesh=mesh,
        in_specs=(
            P(None, "ty", "tx"),
            P(),
            P(),
            P(),
            P(),
            P(),
            P(),
            P(),
            P(),
            P(),
            P(),
            P(),
            P(),
            P(),
            P(),
            P(),
            P(),
            P(),
        ),
        out_specs=P(None, "ty", "tx"),
        check_vma=False,
    )
```

profile of v0, /device:TPU:111, one launch (start us, length us, event | category | flops | bytes accessed | tf_op | source)
XLA Modules:
  0.0 390.8 jit_solution(10242301726044145771)
XLA Ops:
  3.6 5.1 %collective-permute-start = (bf16[9,1,256]{2,0,1:T(8,128)(2,1)S(1)}, bf16[9,1,256]{2,0,1:T(8,128)(2,1)S(1)}, u32[]{:S(2)}, u32[]{:S(2)}) collective-permute-start(bf16[9,1,256]{2,0,1:T(8,128)(2,1)S(1)} %get-tuple-element.50), channel_id=1, source_target_pairs={{0,16},{16,32},{32,48},{48,64},{64,80},{80,96},{96,112},{112,128},... | collective-permute-start | bytes 13832 | tf_op jit(solution)/shard_map/ppermute | solution.py:14
  15.7 4.8 %collective-permute-start.2 = (bf16[9,34,1]{2,0,1:T(8,128)(2,1)S(1)}, bf16[9,34,1]{2,0,1:T(8,128)(2,1)S(1)}, u32[]{:S(2)}, u32[]{:S(2)}) collective-permute-start(bf16[9,34,1]{2,0,1:T(8,128)(2,1)S(1)} %get-tuple-element.43), channel_id=1, source_target_pairs={{0,1},{1,2},{2,3},{3,4},{4,5},{5,6},{6,7},{7,8},{8,9},{9,10},{10,1... | collective-permute-start | bytes 1844 | tf_op jit(solution)/shard_map/ppermute | solution.py:14
  23.1 4.4 %collective-permute-done.3 = bf16[9,34,1]{2,0,1:T(8,128)(2,1)S(1)} collective-permute-done((bf16[9,34,1]{2,0,1:T(8,128)(2,1)S(1)}, bf16[9,34,1]{2,0,1:T(8,128)(2,1)S(1)}, u32[]{:S(2)}, u32[]{:S(2)}) %collective-permute-start.3) | collective-permute-done | bytes 644 | tf_op jit(solution)/shard_map/ppermute | solution.py:15
  30.7 3.4 collective-permute-start.4
  36.3 4.9 %collective-permute-done.5 = bf16[32,1,256]{2,0,1:T(8,128)(2,1)S(1)} collective-permute-done((bf16[32,1,256]{2,0,1:T(8,128)(2,1)S(1)}, bf16[32,1,256]{2,0,1:T(8,128)(2,1)S(1)}, u32[]{:S(2)}, u32[]{:S(2)}) %collective-permute-start.5) | collective-permute-done | bytes 16416 | tf_op jit(solution)/shard_map/ppermute | solution.py:15
  43.8 3.4 collective-permute-start.7
  49.1 3.3 collective-permute-done.7
  56.1 4.8 %reduce_max.36 = bf16[32,16,128]{0,2,1:T(8,128)(2,1)S(1)} reduce(bf16[32,16,2,128,2]{0,4,3,2,1:T(2,128)(2,1)S(1)} %bitcast.794, bf16[]{:T(256)} %constant.26.clone.1), dimensions={2,4}, to_apply=%region_0.1 | reduce | flops 196608 | bytes 655362 | tf_op jit(solution)/shard_map/reduce_max | solution.py:50
  61.1 4.4 %collective-permute-start.8 = (bf16[32,1,128]{2,0,1:T(8,128)(2,1)S(1)}, bf16[32,1,128]{2,0,1:T(8,128)(2,1)S(1)}, u32[]{:S(2)}, u32[]{:S(2)}) collective-permute-start(bf16[32,1,128]{2,0,1:T(8,128)(2,1)S(1)} %get-tuple-element.61), channel_id=1, source_target_pairs={{0,16},{16,32},{32,48},{48,64},{64,80},{80,96},{96,112},{112,128},... | collective-permute-start | bytes 24584 | tf_op jit(solution)/shard_map/ppermute | solution.py:14
  67.8 4.8 %collective-permute-done.9 = bf16[32,1,128]{2,0,1:T(8,128)(2,1)S(1)} collective-permute-done((bf16[32,1,128]{2,0,1:T(8,128)(2,1)S(1)}, bf16[32,1,128]{2,0,1:T(8,128)(2,1)S(1)}, u32[]{:S(2)}, u32[]{:S(2)}) %collective-permute-start.9) | collective-permute-done | bytes 8224 | tf_op jit(solution)/shard_map/ppermute | solution.py:15
  72.8 3.6 collective-permute-start.10
  79.0 4.7 %collective-permute-done.11 = bf16[32,18,1]{2,0,1:T(8,128)(2,1)S(1)} collective-permute-done((bf16[32,18,1]{2,0,1:T(8,128)(2,1)S(1)}, bf16[32,18,1]{2,0,1:T(8,128)(2,1)S(1)}, u32[]{:S(2)}, u32[]{:S(2)}) %collective-permute-start.11) | collective-permute-done | bytes 1184 | tf_op jit(solution)/shard_map/ppermute | solution.py:15
  92.4 5.0 %collective-permute-done.13 = bf16[48,1,64]{2,0,1:T(8,128)(2,1)S(1)} collective-permute-done((bf16[48,1,64]{2,0,1:T(8,128)(2,1)S(1)}, bf16[48,1,64]{2,0,1:T(8,128)(2,1)S(1)}, u32[]{:S(2)}, u32[]{:S(2)}) %collective-permute-start.13) | collective-permute-done | bytes 6176 | tf_op jit(solution)/shard_map/ppermute | solution.py:15
  97.6 3.6 collective-permute-start.14
  103.8 4.3 %collective-permute-done.15 = bf16[48,10,1]{2,0,1:T(8,128)(2,1)S(1)} collective-permute-done((bf16[48,10,1]{2,0,1:T(8,128)(2,1)S(1)}, bf16[48,10,1]{2,0,1:T(8,128)(2,1)S(1)}, u32[]{:S(2)}, u32[]{:S(2)}) %collective-permute-start.15) | collective-permute-done | bytes 992 | tf_op jit(solution)/shard_map/ppermute | solution.py:15
  110.1 3.5 collective-permute-start.16
  115.7 5.0 %collective-permute-done.17 = bf16[64,1,32]{0,2,1:T(8,128)(2,1)S(1)} collective-permute-done((bf16[64,1,32]{0,2,1:T(8,128)(2,1)S(1)}, bf16[64,1,32]{0,2,1:T(8,128)(2,1)S(1)}, u32[]{:S(2)}, u32[]{:S(2)}) %collective-permute-start.17) | collective-permute-done | bytes 4128 | tf_op jit(solution)/shard_map/ppermute | solution.py:15
  122.9 3.1 collective-permute-start.19
  129.4 3.4 collective-permute-start.20
  134.8 5.0 %collective-permute-done.21 = bf16[80,1,16]{0,2,1:T(8,128)(2,1)S(1)} collective-permute-done((bf16[80,1,16]{0,2,1:T(8,128)(2,1)S(1)}, bf16[80,1,16]{0,2,1:T(8,128)(2,1)S(1)}, u32[]{:S(2)}, u32[]{:S(2)}) %collective-permute-start.21) | collective-permute-done | bytes 2592 | tf_op jit(solution)/shard_map/ppermute | solution.py:15
  141.7 3.4 collective-permute-start.23
  148.1 3.4 collective-permute-start.24
  153.5 5.0 %collective-permute-done.25 = bf16[96,1,16]{0,2,1:T(8,128)(2,1)S(1)} collective-permute-done((bf16[96,1,16]{0,2,1:T(8,128)(2,1)S(1)}, bf16[96,1,16]{0,2,1:T(8,128)(2,1)S(1)}, u32[]{:S(2)}, u32[]{:S(2)}) %collective-permute-start.25) | collective-permute-done | bytes 3104 | tf_op jit(solution)/shard_map/ppermute | solution.py:15
  160.4 3.4 collective-permute-start.27
  172.2 5.0 %collective-permute-done.29 = bf16[160,1,32]{0,2,1:T(8,128)(2,1)S(1)} collective-permute-done((bf16[160,1,32]{0,2,1:T(8,128)(2,1)S(1)}, bf16[160,1,32]{0,2,1:T(8,128)(2,1)S(1)}, u32[]{:S(2)}, u32[]{:S(2)}) %collective-permute-start.29) | collective-permute-done | bytes 10272 | tf_op jit(solution)/shard_map/ppermute | solution.py:15
  179.3 3.4 collective-permute-start.31
  191.1 5.0 %collective-permute-done.33 = bf16[112,1,32]{0,2,1:T(8,128)(2,1)S(1)} collective-permute-done((bf16[112,1,32]{0,2,1:T(8,128)(2,1)S(1)}, bf16[112,1,32]{0,2,1:T(8,128)(2,1)S(1)}, u32[]{:S(2)}, u32[]{:S(2)}) %collective-permute-start.33) | collective-permute-done | bytes 7200 | tf_op jit(solution)/shard_map/ppermute | solution.py:15
  198.1 3.4 collective-permute-start.35
  204.8 3.2 collective-permute-start.36
  210.2 5.1 %collective-permute-done.37 = bf16[160,1,64]{0,2,1:T(8,128)(2,1)S(1)} collective-permute-done((bf16[160,1,64]{0,2,1:T(8,128)(2,1)S(1)}, bf16[160,1,64]{0,2,1:T(8,128)(2,1)S(1)}, u32[]{:S(2)}, u32[]{:S(2)}) %collective-permute-start.37) | collective-permute-done | bytes 20512 | tf_op jit(solution)/shard_map/ppermute | solution.py:15
  217.4 3.4 collective-permute-start.39
  224.7 3.3 collective-permute-start.40
  230.1 5.0 %collective-permute-done.41 = bf16[96,1,64]{0,2,1:T(8,128)(2,1)S(1)} collective-permute-done((bf16[96,1,64]{0,2,1:T(8,128)(2,1)S(1)}, bf16[96,1,64]{0,2,1:T(8,128)(2,1)S(1)}, u32[]{:S(2)}, u32[]{:S(2)}) %collective-permute-start.41) | collective-permute-done | bytes 12320 | tf_op jit(solution)/shard_map/ppermute | solution.py:15
  237.1 3.4 collective-permute-start.43
  250.4 4.7 %collective-permute-done.45 = bf16[128,1,128]{2,0,1:T(8,128)(2,1)S(1)} collective-permute-done((bf16[128,1,128]{2,0,1:T(8,128)(2,1)S(1)}, bf16[128,1,128]{2,0,1:T(8,128)(2,1)S(1)}, u32[]{:S(2)}, u32[]{:S(2)}) %collective-permute-start.45) | collective-permute-done | bytes 32800 | tf_op jit(solution)/shard_map/ppermute | solution.py:15
  258.5 4.1 %collective-permute-start.46 = (bf16[128,18,1]{0,1,2:T(8,128)(2,1)S(1)}, bf16[128,18,1]{0,1,2:T(8,128)(2,1)S(1)}, u32[]{:S(2)}, u32[]{:S(2)}) collective-permute-start(bf16[128,18,1]{0,1,2:T(8,128)(2,1)S(1)} %copy.92), channel_id=1, source_target_pairs={{0,1},{1,2},{2,3},{3,4},{4,5},{5,6},{6,7},{7,8},{8,9},{9,10},{10,1... | collective-permute-start | bytes 13832 | tf_op jit(solution)/shard_map/ppermute | solution.py:14
  273.0 5.0 %collective-permute-done.49 = bf16[64,1,128]{2,0,1:T(8,128)(2,1)S(1)} collective-permute-done((bf16[64,1,128]{2,0,1:T(8,128)(2,1)S(1)}, bf16[64,1,128]{2,0,1:T(8,128)(2,1)S(1)}, u32[]{:S(2)}, u32[]{:S(2)}) %collective-permute-start.49) | collective-permute-done | bytes 16416 | tf_op jit(solution)/shard_map/ppermute | solution.py:15
  278.3 5.3 %collective-permute-start.50 = (bf16[64,18,1]{2,0,1:T(8,128)(2,1)S(1)}, bf16[64,18,1]{2,0,1:T(8,128)(2,1)S(1)}, u32[]{:S(2)}, u32[]{:S(2)}) collective-permute-start(bf16[64,18,1]{2,0,1:T(8,128)(2,1)S(1)} %get-tuple-element.41), channel_id=1, source_target_pairs={{0,1},{1,2},{2,3},{3,4},{4,5},{5,6},{6,7},{7,8},{8,9},{9,10},{10,1... | collective-permute-start | bytes 6920 | tf_op jit(solution)/shard_map/ppermute | solution.py:14
  287.2 5.0 %collective-permute-done.51 = bf16[64,18,1]{2,0,1:T(8,128)(2,1)S(1)} collective-permute-done((bf16[64,18,1]{2,0,1:T(8,128)(2,1)S(1)}, bf16[64,18,1]{2,0,1:T(8,128)(2,1)S(1)}, u32[]{:S(2)}, u32[]{:S(2)}) %collective-permute-start.51) | collective-permute-done | bytes 2336 | tf_op jit(solution)/shard_map/ppermute | solution.py:15
  297.3 3.4 collective-permute-start.52
  303.8 4.3 %collective-permute-done.53 = bf16[73,1,256]{2,0,1:T(8,128)(2,1)S(1)} collective-permute-done((bf16[73,1,256]{2,0,1:T(8,128)(2,1)S(1)}, bf16[73,1,256]{2,0,1:T(8,128)(2,1)S(1)}, u32[]{:S(2)}, u32[]{:S(2)}) %collective-permute-start.53) | collective-permute-done | bytes 37408 | tf_op jit(solution)/shard_map/ppermute | solution.py:15
  314.5 4.6 %collective-permute-start.54 = (bf16[73,34,1]{0,1,2:T(8,128)(2,1)S(1)}, bf16[73,34,1]{0,1,2:T(8,128)(2,1)S(1)}, u32[]{:S(2)}, u32[]{:S(2)}) collective-permute-start(bf16[73,34,1]{0,1,2:T(8,128)(2,1)S(1)} %copy.99), channel_id=1, source_target_pairs={{0,1},{1,2},{2,3},{3,4},{4,5},{5,6},{6,7},{7,8},{8,9},{9,10},{10,1... | collective-permute-start | bytes 14900 | tf_op jit(solution)/shard_map/ppermute | solution.py:14
  326.5 3.9 %maximum_maximum_fusion = (bf16[73,34,257]{2,0,1:T(8,128)(2,1)S(1)}, bf16[73,34,257]{2,0,1:T(8,128)(2,1)S(1)}) fusion(bf16[73,1,256]{2,0,1:T(8,128)(2,1)S(1)} %collective-permute-done.53, bf16[9,32,256]{2,0,1:T(8,128)(2,1)S(1)} %copy.61, bf16[64,32,256]{2,0,1:T(8,128)(2,1)S(1)} %copy.97, bf16[73,1,256]{2,0,1:T(8,128)(2,1)S(1)} %collective-permute-done.52, ...), kind=kLoop, calls=%fused_computation.1 | loop fusion | flops 12757480 | bytes 3832208 | tf_op jit(solution)/shard_map/concatenate | solution.py:16
  340.8 4.9 %collective-permute-done.57 = bf16[64,1,256]{2,0,1:T(8,128)(2,1)S(1)} collective-permute-done((bf16[64,1,256]{2,0,1:T(8,128)(2,1)S(1)}, bf16[64,1,256]{2,0,1:T(8,128)(2,1)S(1)}, u32[]{:S(2)}, u32[]{:S(2)}) %collective-permute-start.57) | collective-permute-done | bytes 32800 | tf_op jit(solution)/shard_map/ppermute | solution.py:15
  350.5 4.6 %collective-permute-start.58 = (bf16[64,34,1]{0,1,2:T(8,128)(2,1)S(1)}, bf16[64,34,1]{0,1,2:T(8,128)(2,1)S(1)}, u32[]{:S(2)}, u32[]{:S(2)}) collective-permute-start(bf16[64,34,1]{0,1,2:T(8,128)(2,1)S(1)} %copy.103), channel_id=1, source_target_pairs={{0,1},{1,2},{2,3},{3,4},{4,5},{5,6},{6,7},{7,8},{8,9},{9,10},{10,1... | collective-permute-start | bytes 13064 | tf_op jit(solution)/shard_map/ppermute | solution.py:14
  368.9 5.0 %collective-permute-done.61 = bf16[32,1,256]{2,0,1:T(8,128)(2,1)S(1)} collective-permute-done((bf16[32,1,256]{2,0,1:T(8,128)(2,1)S(1)}, bf16[32,1,256]{2,0,1:T(8,128)(2,1)S(1)}, u32[]{:S(2)}, u32[]{:S(2)}) %collective-permute-start.61) | collective-permute-done | bytes 16416 | tf_op jit(solution)/shard_map/ppermute | solution.py:15
  374.2 4.9 %collective-permute-start.62 = (bf16[32,34,1]{2,0,1:T(8,128)(2,1)S(1)}, bf16[32,34,1]{2,0,1:T(8,128)(2,1)S(1)}, u32[]{:S(2)}, u32[]{:S(2)}) collective-permute-start(bf16[32,34,1]{2,0,1:T(8,128)(2,1)S(1)} %get-tuple-element.23), channel_id=1, source_target_pairs={{0,1},{1,2},{2,3},{3,4},{4,5},{5,6},{6,7},{7,8},{8,9},{9,10},{10,1... | collective-permute-start | bytes 6536 | tf_op jit(solution)/shard_map/ppermute | solution.py:14
  382.6 5.0 %collective-permute-done.63 = bf16[32,34,1]{2,0,1:T(8,128)(2,1)S(1)} collective-permute-done((bf16[32,34,1]{2,0,1:T(8,128)(2,1)S(1)}, bf16[32,34,1]{2,0,1:T(8,128)(2,1)S(1)}, u32[]{:S(2)}, u32[]{:S(2)}) %collective-permute-start.63) | collective-permute-done | bytes 2208 | tf_op jit(solution)/shard_map/ppermute | solution.py:15
  (357 shorter events, 184.1 us)
Async XLA Ops:
  1.0 14.6 %collective-permute-start.1 = (bf16[9,1,256]{2,0,1:T(8,128)(2,1)S(1)}, bf16[9,1,256]{2,0,1:T(8,128)(2,1)S(1)}, u32[]{:S(2)}, u32[]{:S(2)}) collective-permute-start(bf16[9,1,256]{2,0,1:T(8,128)(2,1)S(1)} %get-tuple-element.49), channel_id=1, source_target_pairs={{16,0},{32,16},{48,32},{64,48},{80,64},{96,80},{112,96},{128,112},... | collective-permute-start | bytes 13832 | tf_op jit(solution)/shard_map/ppermute | solution.py:15
  3.6 11.0 %collective-permute-start = (bf16[9,1,256]{2,0,1:T(8,128)(2,1)S(1)}, bf16[9,1,256]{2,0,1:T(8,128)(2,1)S(1)}, u32[]{:S(2)}, u32[]{:S(2)}) collective-permute-start(bf16[9,1,256]{2,0,1:T(8,128)(2,1)S(1)} %get-tuple-element.50), channel_id=1, source_target_pairs={{0,16},{16,32},{32,48},{48,64},{64,80},{80,96},{96,112},{112,128},... | collective-permute-start | bytes 13832 | tf_op jit(solution)/shard_map/ppermute | solution.py:14
  15.7 12.1 %collective-permute-start.2 = (bf16[9,34,1]{2,0,1:T(8,128)(2,1)S(1)}, bf16[9,34,1]{2,0,1:T(8,128)(2,1)S(1)}, u32[]{:S(2)}, u32[]{:S(2)}) collective-permute-start(bf16[9,34,1]{2,0,1:T(8,128)(2,1)S(1)} %get-tuple-element.43), channel_id=1, source_target_pairs={{0,1},{1,2},{2,3},{3,4},{4,5},{5,6},{6,7},{7,8},{8,9},{9,10},{10,1... | collective-permute-start | bytes 1844 | tf_op jit(solution)/shard_map/ppermute | solution.py:14
  20.5 7.0 %collective-permute-start.3 = (bf16[9,34,1]{2,0,1:T(8,128)(2,1)S(1)}, bf16[9,34,1]{2,0,1:T(8,128)(2,1)S(1)}, u32[]{:S(2)}, u32[]{:S(2)}) collective-permute-start(bf16[9,34,1]{2,0,1:T(8,128)(2,1)S(1)} %get-tuple-element.44), channel_id=1, source_target_pairs={{1,0},{2,1},{3,2},{4,3},{5,4},{6,5},{7,6},{8,7},{9,8},{10,9},{11,1... | collective-permute-start | bytes 1844 | tf_op jit(solution)/shard_map/ppermute | solution.py:15
  30.7 5.6 %collective-permute-start.4 = (bf16[32,1,256]{2,0,1:T(8,128)(2,1)S(1)}, bf16[32,1,256]{2,0,1:T(8,128)(2,1)S(1)}, u32[]{:S(2)}, u32[]{:S(2)}) collective-permute-start(bf16[32,1,256]{2,0,1:T(8,128)(2,1)S(1)} %get-tuple-element.33), channel_id=1, source_target_pairs={{0,16},{16,32},{32,48},{48,64},{64,80},{80,96},{96,112},{112,128},... | collective-permute-start | bytes 49160 | tf_op jit(solution)/shard_map/ppermute | solution.py:14
  34.1 7.2 %collective-permute-start.5 = (bf16[32,1,256]{2,0,1:T(8,128)(2,1)S(1)}, bf16[32,1,256]{2,0,1:T(8,128)(2,1)S(1)}, u32[]{:S(2)}, u32[]{:S(2)}) collective-permute-start(bf16[32,1,256]{2,0,1:T(8,128)(2,1)S(1)} %get-tuple-element.34), channel_id=1, source_target_pairs={{16,0},{32,16},{48,32},{64,48},{80,64},{96,80},{112,96},{128,112},... | collective-permute-start | bytes 49160 | tf_op jit(solution)/shard_map/ppermute | solution.py:15
  41.5 7.6 %collective-permute-start.6 = (bf16[32,34,1]{2,0,1:T(8,128)(2,1)S(1)}, bf16[32,34,1]{2,0,1:T(8,128)(2,1)S(1)}, u32[]{:S(2)}, u32[]{:S(2)}) collective-permute-start(bf16[32,34,1]{2,0,1:T(8,128)(2,1)S(1)} %get-tuple-element.27), channel_id=1, source_target_pairs={{0,1},{1,2},{2,3},{3,4},{4,5},{5,6},{6,7},{7,8},{8,9},{9,10},{10,1... | collective-permute-start | bytes 6536 | tf_op jit(solution)/shard_map/ppermute | solution.py:14
  43.8 8.5 %collective-permute-start.7 = (bf16[32,34,1]{2,0,1:T(8,128)(2,1)S(1)}, bf16[32,34,1]{2,0,1:T(8,128)(2,1)S(1)}, u32[]{:S(2)}, u32[]{:S(2)}) collective-permute-start(bf16[32,34,1]{2,0,1:T(8,128)(2,1)S(1)} %get-tuple-element.28), channel_id=1, source_target_pairs={{1,0},{2,1},{3,2},{4,3},{5,4},{6,5},{7,6},{8,7},{9,8},{10,9},{11,1... | collective-permute-start | bytes 6536 | tf_op jit(solution)/shard_map/ppermute | solution.py:15
  61.1 6.7 %collective-permute-start.8 = (bf16[32,1,128]{2,0,1:T(8,128)(2,1)S(1)}, bf16[32,1,128]{2,0,1:T(8,128)(2,1)S(1)}, u32[]{:S(2)}, u32[]{:S(2)}) collective-permute-start(bf16[32,1,128]{2,0,1:T(8,128)(2,1)S(1)} %get-tuple-element.61), channel_id=1, source_target_pairs={{0,16},{16,32},{32,48},{48,64},{64,80},{80,96},{96,112},{112,128},... | collective-permute-start | bytes 24584 | tf_op jit(solution)/shard_map/ppermute | solution.py:14
  65.6 7.1 %collective-permute-start.9 = (bf16[32,1,128]{2,0,1:T(8,128)(2,1)S(1)}, bf16[32,1,128]{2,0,1:T(8,128)(2,1)S(1)}, u32[]{:S(2)}, u32[]{:S(2)}) collective-permute-start(bf16[32,1,128]{2,0,1:T(8,128)(2,1)S(1)} %get-tuple-element.62), channel_id=1, source_target_pairs={{16,0},{32,16},{48,32},{64,48},{80,64},{96,80},{112,96},{128,112},... | collective-permute-start | bytes 24584 | tf_op jit(solution)/shard_map/ppermute | solution.py:15
  72.8 6.2 %collective-permute-start.10 = (bf16[32,18,1]{2,0,1:T(8,128)(2,1)S(1)}, bf16[32,18,1]{2,0,1:T(8,128)(2,1)S(1)}, u32[]{:S(2)}, u32[]{:S(2)}) collective-permute-start(bf16[32,18,1]{2,0,1:T(8,128)(2,1)S(1)} %get-tuple-element.57), channel_id=1, source_target_pairs={{0,1},{1,2},{2,3},{3,4},{4,5},{5,6},{6,7},{7,8},{8,9},{9,10},{10,1... | collective-permute-start | bytes 3464 | tf_op jit(solution)/shard_map/ppermute | solution.py:14
  76.3 7.4 %collective-permute-start.11 = (bf16[32,18,1]{2,0,1:T(8,128)(2,1)S(1)}, bf16[32,18,1]{2,0,1:T(8,128)(2,1)S(1)}, u32[]{:S(2)}, u32[]{:S(2)}) collective-permute-start(bf16[32,18,1]{2,0,1:T(8,128)(2,1)S(1)} %get-tuple-element.58), channel_id=1, source_target_pairs={{1,0},{2,1},{3,2},{4,3},{5,4},{6,5},{7,6},{8,7},{9,8},{10,9},{11,1... | collective-permute-start | bytes 3464 | tf_op jit(solution)/shard_map/ppermute | solution.py:15
  90.3 7.1 %collective-permute-start.13 = (bf16[48,1,64]{2,0,1:T(8,128)(2,1)S(1)}, bf16[48,1,64]{2,0,1:T(8,128)(2,1)S(1)}, u32[]{:S(2)}, u32[]{:S(2)}) collective-permute-start(bf16[48,1,64]{2,0,1:T(8,128)(2,1)S(1)} %get-tuple-element.72), channel_id=1, source_target_pairs={{16,0},{32,16},{48,32},{64,48},{80,64},{96,80},{112,96},{128,112},... | collective-permute-start | bytes 18440 | tf_op jit(solution)/shard_map/ppermute | solution.py:15
  97.6 6.2 %collective-permute-start.14 = (bf16[48,10,1]{2,0,1:T(8,128)(2,1)S(1)}, bf16[48,10,1]{2,0,1:T(8,128)(2,1)S(1)}, u32[]{:S(2)}, u32[]{:S(2)}) collective-permute-start(bf16[48,10,1]{2,0,1:T(8,128)(2,1)S(1)} %get-tuple-element.65), channel_id=1, source_target_pairs={{0,1},{1,2},{2,3},{3,4},{4,5},{5,6},{6,7},{7,8},{8,9},{9,10},{10,1... | collective-permute-start | bytes 2888 | tf_op jit(solution)/shard_map/ppermute | solution.py:14
  101.2 6.8 %collective-permute-start.15 = (bf16[48,10,1]{2,0,1:T(8,128)(2,1)S(1)}, bf16[48,10,1]{2,0,1:T(8,128)(2,1)S(1)}, u32[]{:S(2)}, u32[]{:S(2)}) collective-permute-start(bf16[48,10,1]{2,0,1:T(8,128)(2,1)S(1)} %get-tuple-element.66), channel_id=1, source_target_pairs={{1,0},{2,1},{3,2},{4,3},{5,4},{6,5},{7,6},{8,7},{9,8},{10,9},{11,1... | collective-permute-start | bytes 2888 | tf_op jit(solution)/shard_map/ppermute | solution.py:15
  110.1 5.6 %collective-permute-start.16 = (bf16[64,1,32]{0,2,1:T(8,128)(2,1)S(1)}, bf16[64,1,32]{0,2,1:T(8,128)(2,1)S(1)}, u32[]{:S(2)}, u32[]{:S(2)}) collective-permute-start(bf16[64,1,32]{0,2,1:T(8,128)(2,1)S(1)} %get-tuple-element.85), channel_id=1, source_target_pairs={{0,16},{16,32},{32,48},{48,64},{64,80},{80,96},{96,112},{112,128},... | collective-permute-start | bytes 12296 | tf_op jit(solution)/shard_map/ppermute | solution.py:14
  113.6 7.1 %collective-permute-start.17 = (bf16[64,1,32]{0,2,1:T(8,128)(2,1)S(1)}, bf16[64,1,32]{0,2,1:T(8,128)(2,1)S(1)}, u32[]{:S(2)}, u32[]{:S(2)}) collective-permute-start(bf16[64,1,32]{0,2,1:T(8,128)(2,1)S(1)} %get-tuple-element.86), channel_id=1, source_target_pairs={{16,0},{32,16},{48,32},{64,48},{80,64},{96,80},{112,96},{128,112},... | collective-permute-start | bytes 12296 | tf_op jit(solution)/shard_map/ppermute | solution.py:15
  120.7 5.6 %collective-permute-start.18 = (bf16[64,6,1]{0,2,1:T(2,128)(2,1)S(1)}, bf16[64,6,1]{0,2,1:T(2,128)(2,1)S(1)}, u32[]{:S(2)}, u32[]{:S(2)}) collective-permute-start(bf16[64,6,1]{0,2,1:T(2,128)(2,1)S(1)} %get-tuple-element.81), channel_id=1, source_target_pairs={{0,1},{1,2},{2,3},{3,4},{4,5},{5,6},{6,7},{7,8},{8,9},{9,10},{10,1... | collective-permute-start | bytes 2312 | tf_op jit(solution)/shard_map/ppermute | solution.py:14
  132.7 7.0 %collective-permute-start.21 = (bf16[80,1,16]{0,2,1:T(8,128)(2,1)S(1)}, bf16[80,1,16]{0,2,1:T(8,128)(2,1)S(1)}, u32[]{:S(2)}, u32[]{:S(2)}) collective-permute-start(bf16[80,1,16]{0,2,1:T(8,128)(2,1)S(1)} %get-tuple-element.120), channel_id=1, source_target_pairs={{16,0},{32,16},{48,32},{64,48},{80,64},{96,80},{112,96},{128,112},... | collective-permute-start | bytes 7688 | tf_op jit(solution)/shard_map/ppermute | solution.py:15
  151.5 7.0 %collective-permute-start.25 = (bf16[96,1,16]{0,2,1:T(8,128)(2,1)S(1)}, bf16[96,1,16]{0,2,1:T(8,128)(2,1)S(1)}, u32[]{:S(2)}, u32[]{:S(2)}) collective-permute-start(bf16[96,1,16]{0,2,1:T(8,128)(2,1)S(1)} %get-tuple-element.118), channel_id=1, source_target_pairs={{16,0},{32,16},{48,32},{64,48},{80,64},{96,80},{112,96},{128,112},... | collective-permute-start | bytes 9224 | tf_op jit(solution)/shard_map/ppermute | solution.py:15
  158.5 5.6 %collective-permute-start.26 = (bf16[96,4,1]{0,2,1:T(2,128)(2,1)S(1)}, bf16[96,4,1]{0,2,1:T(2,128)(2,1)S(1)}, u32[]{:S(2)}, u32[]{:S(2)}) collective-permute-start(bf16[96,4,1]{0,2,1:T(2,128)(2,1)S(1)} %get-tuple-element.98), channel_id=1, source_target_pairs={{0,1},{1,2},{2,3},{3,4},{4,5},{5,6},{6,7},{7,8},{8,9},{9,10},{10,1... | collective-permute-start | bytes 2312 | tf_op jit(solution)/shard_map/ppermute | solution.py:14
  170.1 7.2 %collective-permute-start.29 = (bf16[160,1,32]{0,2,1:T(8,128)(2,1)S(1)}, bf16[160,1,32]{0,2,1:T(8,128)(2,1)S(1)}, u32[]{:S(2)}, u32[]{:S(2)}) collective-permute-start(bf16[160,1,32]{0,2,1:T(8,128)(2,1)S(1)} %get-tuple-element.74), channel_id=1, source_target_pairs={{16,0},{32,16},{48,32},{64,48},{80,64},{96,80},{112,96},{128,112},... | collective-permute-start | bytes 30728 | tf_op jit(solution)/shard_map/ppermute | solution.py:15
  177.3 5.7 %collective-permute-start.30 = (bf16[160,6,1]{0,2,1:T(2,128)(2,1)S(1)}, bf16[160,6,1]{0,2,1:T(2,128)(2,1)S(1)}, u32[]{:S(2)}, u32[]{:S(2)}) collective-permute-start(bf16[160,6,1]{0,2,1:T(2,128)(2,1)S(1)} %get-tuple-element.69), channel_id=1, source_target_pairs={{0,1},{1,2},{2,3},{3,4},{4,5},{5,6},{6,7},{7,8},{8,9},{9,10},{10,1... | collective-permute-start | bytes 5768 | tf_op jit(solution)/shard_map/ppermute | solution.py:14
  179.3 5.6 %collective-permute-start.31 = (bf16[160,6,1]{0,2,1:T(2,128)(2,1)S(1)}, bf16[160,6,1]{0,2,1:T(2,128)(2,1)S(1)}, u32[]{:S(2)}, u32[]{:S(2)}) collective-permute-start(bf16[160,6,1]{0,2,1:T(2,128)(2,1)S(1)} %get-tuple-element.70), channel_id=1, source_target_pairs={{1,0},{2,1},{3,2},{4,3},{5,4},{6,5},{7,6},{8,7},{9,8},{10,9},{11,1... | collective-permute-start | bytes 5768 | tf_op jit(solution)/shard_map/ppermute | solution.py:15
  189.0 7.1 %collective-permute-start.33 = (bf16[112,1,32]{0,2,1:T(8,128)(2,1)S(1)}, bf16[112,1,32]{0,2,1:T(8,128)(2,1)S(1)}, u32[]{:S(2)}, u32[]{:S(2)}) collective-permute-start(bf16[112,1,32]{0,2,1:T(8,128)(2,1)S(1)} %get-tuple-element.84), channel_id=1, source_target_pairs={{16,0},{32,16},{48,32},{64,48},{80,64},{96,80},{112,96},{128,112},... | collective-permute-start | bytes 21512 | tf_op jit(solution)/shard_map/ppermute | solution.py:15
  196.1 5.6 %collective-permute-start.34 = (bf16[112,6,1]{0,2,1:T(2,128)(2,1)S(1)}, bf16[112,6,1]{0,2,1:T(2,128)(2,1)S(1)}, u32[]{:S(2)}, u32[]{:S(2)}) collective-permute-start(bf16[112,6,1]{0,2,1:T(2,128)(2,1)S(1)} %get-tuple-element.77), channel_id=1, source_target_pairs={{0,1},{1,2},{2,3},{3,4},{4,5},{5,6},{6,7},{7,8},{8,9},{9,10},{10,1... | collective-permute-start | bytes 4040 | tf_op jit(solution)/shard_map/ppermute | solution.py:14
  208.0 7.3 %collective-permute-start.37 = (bf16[160,1,64]{0,2,1:T(8,128)(2,1)S(1)}, bf16[160,1,64]{0,2,1:T(8,128)(2,1)S(1)}, u32[]{:S(2)}, u32[]{:S(2)}) collective-permute-start(bf16[160,1,64]{0,2,1:T(8,128)(2,1)S(1)} %get-tuple-element.48), channel_id=1, source_target_pairs={{16,0},{32,16},{48,32},{64,48},{80,64},{96,80},{112,96},{128,112},... | collective-permute-start | bytes 61448 | tf_op jit(solution)/shard_map/ppermute | solution.py:15
  215.4 5.9 %collective-permute-start.38 = (bf16[160,10,1]{0,2,1:T(2,128)(2,1)S(1)}, bf16[160,10,1]{0,2,1:T(2,128)(2,1)S(1)}, u32[]{:S(2)}, u32[]{:S(2)}) collective-permute-start(bf16[160,10,1]{0,2,1:T(2,128)(2,1)S(1)} %get-tuple-element.37), channel_id=1, source_target_pairs={{0,1},{1,2},{2,3},{3,4},{4,5},{5,6},{6,7},{7,8},{8,9},{9,10},{10,1... | collective-permute-start | bytes 9608 | tf_op jit(solution)/shard_map/ppermute | solution.py:14
  217.4 5.6 %collective-permute-start.39 = (bf16[160,10,1]{0,2,1:T(2,128)(2,1)S(1)}, bf16[160,10,1]{0,2,1:T(2,128)(2,1)S(1)}, u32[]{:S(2)}, u32[]{:S(2)}) collective-permute-start(bf16[160,10,1]{0,2,1:T(2,128)(2,1)S(1)} %get-tuple-element.38), channel_id=1, source_target_pairs={{1,0},{2,1},{3,2},{4,3},{5,4},{6,5},{7,6},{8,7},{9,8},{10,9},{11,1... | collective-permute-start | bytes 9608 | tf_op jit(solution)/shard_map/ppermute | solution.py:15
  228.0 7.2 %collective-permute-start.41 = (bf16[96,1,64]{0,2,1:T(8,128)(2,1)S(1)}, bf16[96,1,64]{0,2,1:T(8,128)(2,1)S(1)}, u32[]{:S(2)}, u32[]{:S(2)}) collective-permute-start(bf16[96,1,64]{0,2,1:T(8,128)(2,1)S(1)} %get-tuple-element.60), channel_id=1, source_target_pairs={{16,0},{32,16},{48,32},{64,48},{80,64},{96,80},{112,96},{128,112},... | collective-permute-start | bytes 36872 | tf_op jit(solution)/shard_map/ppermute | solution.py:15
  235.2 5.7 %collective-permute-start.42 = (bf16[96,10,1]{0,2,1:T(2,128)(2,1)S(1)}, bf16[96,10,1]{0,2,1:T(2,128)(2,1)S(1)}, u32[]{:S(2)}, u32[]{:S(2)}) collective-permute-start(bf16[96,10,1]{0,2,1:T(2,128)(2,1)S(1)} %get-tuple-element.53), channel_id=1, source_target_pairs={{0,1},{1,2},{2,3},{3,4},{4,5},{5,6},{6,7},{7,8},{8,9},{9,10},{10,1... | collective-permute-start | bytes 5768 | tf_op jit(solution)/shard_map/ppermute | solution.py:14
  237.1 5.6 %collective-permute-start.43 = (bf16[96,10,1]{0,2,1:T(2,128)(2,1)S(1)}, bf16[96,10,1]{0,2,1:T(2,128)(2,1)S(1)}, u32[]{:S(2)}, u32[]{:S(2)}) collective-permute-start(bf16[96,10,1]{0,2,1:T(2,128)(2,1)S(1)} %get-tuple-element.54), channel_id=1, source_target_pairs={{1,0},{2,1},{3,2},{4,3},{5,4},{6,5},{7,6},{8,7},{9,8},{10,9},{11,1... | collective-permute-start | bytes 5768 | tf_op jit(solution)/shard_map/ppermute | solution.py:15
  244.6 5.8 %collective-permute-start.44 = (bf16[128,1,128]{2,0,1:T(8,128)(2,1)S(1)}, bf16[128,1,128]{2,0,1:T(8,128)(2,1)S(1)}, u32[]{:S(2)}, u32[]{:S(2)}) collective-permute-start(bf16[128,1,128]{2,0,1:T(8,128)(2,1)S(1)} %get-tuple-element.31), channel_id=1, source_target_pairs={{0,16},{16,32},{32,48},{48,64},{64,80},{80,96},{96,112},{112,128},... | collective-permute-start | bytes 98312 | tf_op jit(solution)/shard_map/ppermute | solution.py:14
  247.7 7.3 %collective-permute-start.45 = (bf16[128,1,128]{2,0,1:T(8,128)(2,1)S(1)}, bf16[128,1,128]{2,0,1:T(8,128)(2,1)S(1)}, u32[]{:S(2)}, u32[]{:S(2)}) collective-permute-start(bf16[128,1,128]{2,0,1:T(8,128)(2,1)S(1)} %get-tuple-element.32), channel_id=1, source_target_pairs={{16,0},{32,16},{48,32},{64,48},{80,64},{96,80},{112,96},{128,112},... | collective-permute-start | bytes 98312 | tf_op jit(solution)/shard_map/ppermute | solution.py:15
  256.0 7.6 %collective-permute-start.47 = (bf16[128,18,1]{0,1,2:T(8,128)(2,1)S(1)}, bf16[128,18,1]{0,1,2:T(8,128)(2,1)S(1)}, u32[]{:S(2)}, u32[]{:S(2)}) collective-permute-start(bf16[128,18,1]{0,1,2:T(8,128)(2,1)S(1)} %copy.94), channel_id=1, source_target_pairs={{1,0},{2,1},{3,2},{4,3},{5,4},{6,5},{7,6},{8,7},{9,8},{10,9},{11,1... | collective-permute-start | bytes 13832 | tf_op jit(solution)/shard_map/ppermute | solution.py:15
  270.9 7.2 %collective-permute-start.49 = (bf16[64,1,128]{2,0,1:T(8,128)(2,1)S(1)}, bf16[64,1,128]{2,0,1:T(8,128)(2,1)S(1)}, u32[]{:S(2)}, u32[]{:S(2)}) collective-permute-start(bf16[64,1,128]{2,0,1:T(8,128)(2,1)S(1)} %get-tuple-element.46), channel_id=1, source_target_pairs={{16,0},{32,16},{48,32},{64,48},{80,64},{96,80},{112,96},{128,112},... | collective-permute-start | bytes 49160 | tf_op jit(solution)/shard_map/ppermute | solution.py:15
  278.3 9.0 %collective-permute-start.50 = (bf16[64,18,1]{2,0,1:T(8,128)(2,1)S(1)}, bf16[64,18,1]{2,0,1:T(8,128)(2,1)S(1)}, u32[]{:S(2)}, u32[]{:S(2)}) collective-permute-start(bf16[64,18,1]{2,0,1:T(8,128)(2,1)S(1)} %get-tuple-element.41), channel_id=1, source_target_pairs={{0,1},{1,2},{2,3},{3,4},{4,5},{5,6},{6,7},{7,8},{8,9},{9,10},{10,1... | collective-permute-start | bytes 6920 | tf_op jit(solution)/shard_map/ppermute | solution.py:14
  283.6 8.7 %collective-permute-start.51 = (bf16[64,18,1]{2,0,1:T(8,128)(2,1)S(1)}, bf16[64,18,1]{2,0,1:T(8,128)(2,1)S(1)}, u32[]{:S(2)}, u32[]{:S(2)}) collective-permute-start(bf16[64,18,1]{2,0,1:T(8,128)(2,1)S(1)} %get-tuple-element.42), channel_id=1, source_target_pairs={{1,0},{2,1},{3,2},{4,3},{5,4},{6,5},{7,6},{8,7},{9,8},{10,9},{11,1... | collective-permute-start | bytes 6920 | tf_op jit(solution)/shard_map/ppermute | solution.py:15
  297.3 6.4 %collective-permute-start.52 = (bf16[73,1,256]{2,0,1:T(8,128)(2,1)S(1)}, bf16[73,1,256]{2,0,1:T(8,128)(2,1)S(1)}, u32[]{:S(2)}, u32[]{:S(2)}) collective-permute-start(bf16[73,1,256]{2,0,1:T(8,128)(2,1)S(1)} %get-tuple-element.9), channel_id=1, source_target_pairs={{0,16},{16,32},{32,48},{48,64},{64,80},{80,96},{96,112},{112,128},... | collective-permute-start | bytes 112136 | tf_op jit(solution)/shard_map/ppermute | solution.py:14
  300.7 7.4 %collective-permute-start.53 = (bf16[73,1,256]{2,0,1:T(8,128)(2,1)S(1)}, bf16[73,1,256]{2,0,1:T(8,128)(2,1)S(1)}, u32[]{:S(2)}, u32[]{:S(2)}) collective-permute-start(bf16[73,1,256]{2,0,1:T(8,128)(2,1)S(1)} %get-tuple-element.10), channel_id=1, source_target_pairs={{16,0},{32,16},{48,32},{64,48},{80,64},{96,80},{112,96},{128,112},... | collective-permute-start | bytes 112136 | tf_op jit(solution)/shard_map/ppermute | solution.py:15
  312.6 12.7 %collective-permute-start.55 = (bf16[73,34,1]{0,1,2:T(8,128)(2,1)S(1)}, bf16[73,34,1]{0,1,2:T(8,128)(2,1)S(1)}, u32[]{:S(2)}, u32[]{:S(2)}) collective-permute-start(bf16[73,34,1]{0,1,2:T(8,128)(2,1)S(1)} %copy.101), channel_id=1, source_target_pairs={{1,0},{2,1},{3,2},{4,3},{5,4},{6,5},{7,6},{8,7},{9,8},{10,9},{11,1... | collective-permute-start | bytes 14900 | tf_op jit(solution)/shard_map/ppermute | solution.py:15
  314.5 9.5 %collective-permute-start.54 = (bf16[73,34,1]{0,1,2:T(8,128)(2,1)S(1)}, bf16[73,34,1]{0,1,2:T(8,128)(2,1)S(1)}, u32[]{:S(2)}, u32[]{:S(2)}) collective-permute-start(bf16[73,34,1]{0,1,2:T(8,128)(2,1)S(1)} %copy.99), channel_id=1, source_target_pairs={{0,1},{1,2},{2,3},{3,4},{4,5},{5,6},{6,7},{7,8},{8,9},{9,10},{10,1... | collective-permute-start | bytes 14900 | tf_op jit(solution)/shard_map/ppermute | solution.py:14
  338.3 7.3 %collective-permute-start.57 = (bf16[64,1,256]{2,0,1:T(8,128)(2,1)S(1)}, bf16[64,1,256]{2,0,1:T(8,128)(2,1)S(1)}, u32[]{:S(2)}, u32[]{:S(2)}) collective-permute-start(bf16[64,1,256]{2,0,1:T(8,128)(2,1)S(1)} %get-tuple-element.16), channel_id=1, source_target_pairs={{16,0},{32,16},{48,32},{64,48},{80,64},{96,80},{112,96},{128,112},... | collective-permute-start | bytes 98312 | tf_op jit(solution)/shard_map/ppermute | solution.py:15
  348.6 9.2 %collective-permute-start.59 = (bf16[64,34,1]{0,1,2:T(8,128)(2,1)S(1)}, bf16[64,34,1]{0,1,2:T(8,128)(2,1)S(1)}, u32[]{:S(2)}, u32[]{:S(2)}) collective-permute-start(bf16[64,34,1]{0,1,2:T(8,128)(2,1)S(1)} %copy.105), channel_id=1, source_target_pairs={{1,0},{2,1},{3,2},{4,3},{5,4},{6,5},{7,6},{8,7},{9,8},{10,9},{11,1... | collective-permute-start | bytes 13064 | tf_op jit(solution)/shard_map/ppermute | solution.py:15
  350.5 6.1 %collective-permute-start.58 = (bf16[64,34,1]{0,1,2:T(8,128)(2,1)S(1)}, bf16[64,34,1]{0,1,2:T(8,128)(2,1)S(1)}, u32[]{:S(2)}, u32[]{:S(2)}) collective-permute-start(bf16[64,34,1]{0,1,2:T(8,128)(2,1)S(1)} %copy.103), channel_id=1, source_target_pairs={{0,1},{1,2},{2,3},{3,4},{4,5},{5,6},{6,7},{7,8},{8,9},{9,10},{10,1... | collective-permute-start | bytes 13064 | tf_op jit(solution)/shard_map/ppermute | solution.py:14
  366.8 7.2 %collective-permute-start.61 = (bf16[32,1,256]{2,0,1:T(8,128)(2,1)S(1)}, bf16[32,1,256]{2,0,1:T(8,128)(2,1)S(1)}, u32[]{:S(2)}, u32[]{:S(2)}) collective-permute-start(bf16[32,1,256]{2,0,1:T(8,128)(2,1)S(1)} %get-tuple-element.30), channel_id=1, source_target_pairs={{16,0},{32,16},{48,32},{64,48},{80,64},{96,80},{112,96},{128,112},... | collective-permute-start | bytes 49160 | tf_op jit(solution)/shard_map/ppermute | solution.py:15
  374.2 8.4 %collective-permute-start.62 = (bf16[32,34,1]{2,0,1:T(8,128)(2,1)S(1)}, bf16[32,34,1]{2,0,1:T(8,128)(2,1)S(1)}, u32[]{:S(2)}, u32[]{:S(2)}) collective-permute-start(bf16[32,34,1]{2,0,1:T(8,128)(2,1)S(1)} %get-tuple-element.23), channel_id=1, source_target_pairs={{0,1},{1,2},{2,3},{3,4},{4,5},{5,6},{6,7},{7,8},{8,9},{9,10},{10,1... | collective-permute-start | bytes 6536 | tf_op jit(solution)/shard_map/ppermute | solution.py:14
  379.1 8.5 %collective-permute-start.63 = (bf16[32,34,1]{2,0,1:T(8,128)(2,1)S(1)}, bf16[32,34,1]{2,0,1:T(8,128)(2,1)S(1)}, u32[]{:S(2)}, u32[]{:S(2)}) collective-permute-start(bf16[32,34,1]{2,0,1:T(8,128)(2,1)S(1)} %get-tuple-element.24), channel_id=1, source_target_pairs={{1,0},{2,1},{3,2},{4,3},{5,4},{6,5},{7,6},{8,7},{9,8},{10,9},{11,1... | collective-permute-start | bytes 6536 | tf_op jit(solution)/shard_map/ppermute | solution.py:15
  (35 other events, 335.2 us)
where the time goes:
time: 397 us; the launch traced here: 391 us
  starting transfers between devices  179 us (45%)
  waiting for transfers between devices  118 us (30%)
  matrix products  42.6 us (11%)
  local copies, waits for them, and re-layouts  31 us (8%)
  other arithmetic  17.5 us (4%)
    ppermute x32, waiting for transfers between devices, with_halo(): after = lax.ppermute(initial, axis, down)  114 us
    ppermute x32, starting transfers between devices, with_halo(): before = lax.ppermute(last, axis, up)  105 us
    ppermute x32, starting transfers between devices, with_halo(): after = lax.ppermute(initial, axis, down)  74.4 us
    dot_general x144, matrix products, convolve_tile(): jnp.einsum('oc,chw->ohw', weight[row_off, col_off], padded[:, row_off:row...  42.6 us
    concatenate x23, other arithmetic, with_halo(): array = jnp.concatenate([before, array, after], axis=dim)  10.7 us
  transfers between devices with their start and end apart: 64, of which 33 were waited for; matrix products, arithmetic and copies ran while one was open for 7% of the time, Pallas kernels for 0%

commit v1 on v0

v1 whole, which is shorter than its diff:
```python
import functools

import jax
import jax.numpy as jnp
from jax import lax
from jax.experimental import pallas as pl
from jax.experimental.pallas import tpu as pltpu
from jax.sharding import PartitionSpec as P

F32 = jnp.float32
BF = jnp.bfloat16
BIG = 3.0e38
MESH = pl.DeviceIdType.MESH

COUT = [32, 32, 48, 64, 80, 96, 96, 112, 112, 96, 96, 64, 64, 64, 32, 3]
CIN = [9, 32, 32, 48, 64, 80, 96, 160, 112, 160, 96, 128, 64, 73, 64, 32]
NP = [32, 32, 64, 64, 128, 128, 128, 128, 128, 128, 128, 64, 64, 64, 32, 4]
KDIM = [256, 512, 512, 1024, 1024, 2048, 2048, 1536, 2048, 1536, 2048, 1024, 1024, 512, 1024, 512]
DIRS = [(dy, dx) for dy in (-1, 0, 1) for dx in (-1, 0, 1) if (dy, dx) != (0, 0)]
FAR = DIRS + [(dy, dx) for dy in (-3, -2, 2, 3) for dx in (-1, 0, 1)]

SCRATCH = dict(
    rows_in=((2, 9, 32, 256), BF),
    cols_out=((2, 80, 128), BF),
    cols_in=((6, 80, 128), BF),
    tile_out=((64, 128), BF),
    tiles_in=((20, 64, 128), BF),
    ext_side=((9, 96, 128), F32),
    ext=((9, 96, 384), BF),
    spread=((384, 1024), BF),
    planar=((8, 16 * 96, 128), F32),
    rows_yc=((72, 16, 1024), BF),
    eye=((160, 256), BF),
    fwin=((40, 160, 256), BF),
    s1=((36, 160, 256), BF),
    pix1=((34, 176, 128), F32),
    s2=((17, 80, 256), BF),
    pix2=((16, 112, 128), F32),
    s3=((5, 48, 512), BF),
    pix3o=((4, 48, 128), F32),
    pix3=((28, 112, 128), F32),
    s4=((11, 32, 512), BF),
    pix4=((10, 48, 128), F32),
    s5=((5, 16, 1024), BF),
    s6=((4, 16, 1024), BF),
    r7=((6, 32, 256), BF),
    k7=((6, 32, 512), BF),
    s8=((5, 32, 1024), BF),
    r9=((8, 48, 256), BF),
    k9=((8, 48, 512), BF),
    s10=((7, 48, 1024), BF),
    r11=((12, 80, 256), BF),
    k11=((12, 80, 256), BF),
    s12=((11, 80, 512), BF),
    r13=((24, 144, 128), BF),
    s14=((21, 144, 512), BF),
    s15=((20, 144, 256), BF),
    t128=((968, 128), F32),
    t256=((968, 256), F32),
    t512=((360, 512), F32),
    td=((20, 184, 128), F32),
    cap128=((160, 128), F32),
    cap256=((144, 256), F32),
    cap512=((48, 512), F32),
    w15f=((16, 512), F32),
    z0=((144, 144), F32),
    z1=((144, 144), F32),
    zf=((2, 144, 128), F32),
    out32=((6, 32, 128), F32),
)
for _k in range(16):
    SCRATCH["w%d" % _k] = ((16 if _k == 15 else 4 * NP[_k], KDIM[_k]), BF)


def iota(shape, dim):
    return lax.broadcasted_iota(jnp.int32, shape, dim)


def nt(a, b):
    return lax.dot_general(a, b, (((1,), (1,)), ((), ())), preferred_element_type=F32)


def replicated_taps(w, number, first, count, period):
    cin = CIN[number]
    row = iota((cin, 128), 0)
    lane = iota((cin, 128), 1)
    pick = ((row - first == lane % period) & (row >= first) & (row < first + count)).astype(F32).astype(BF)
    return [
        [jnp.dot(w[ky, kx], pick, preferred_element_type=F32) for kx in range(3)] for ky in range(3)
    ]


def choose(groups, period, rows):
    lane = iota((rows, 128), 1)
    value = jnp.zeros((rows, 128), F32)
    for place, tap in enumerate(groups):
        if tap is not None:
            value = jnp.where((lane >= place * period) & (lane < (place + 1) * period), tap, value)
    return value


def tap_of(taps, r, s, qy, qx):
    ky, kx = r - qy, s - qx
    if 0 <= ky < 3 and 0 <= kx < 3:
        return taps[ky][kx]
    return None


def prepare_blocks(wt, w, number, offset, first, count, lanes):
    cout, np_ = COUT[number], NP[number]
    if lanes == 128:
        for ky in range(3):
            for kx in range(3):
                tap = w[ky, kx]
                for qy in range(2):
                    for qx in range(2):
                        r, s = ky + qy, kx + qx
                        t, py, u, px = r // 2, r % 2, s // 2, s % 2
                        k = offset + ((t * 2 + u) * 4 + py * 2 + px) * 128
                        n = (qy * 2 + qx) * np_
                        wt[n : n + cout, k : k + count] = tap
        return
    taps = replicated_taps(w, number, first, count, lanes)
    per = 128 // lanes
    for qy in range(2):
        for qx in range(2):
            n = (qy * 2 + qx) * np_
            for t in range(2):
                for u in range(2):
                    places = [tap_of(taps, 2 * t + py, 2 * u + px, qy, qx) for py in range(2) for px in range(2)]
                    for chunk in range(4 // per):
                        k = offset + (t * 2 + u) * 4 * lanes + chunk * 128
                        value = choose(places[chunk * per : (chunk + 1) * per], lanes, cout)
                        wt[n : n + cout, k : k + 128] = value.astype(BF)


def prepare_window(wt, w, number, offset, first):
    cout, np_ = COUT[number], NP[number]
    taps = replicated_taps(w, number, first, 9, 16)
    for qy in range(2):
        for qx in range(2):
            n = (qy * 2 + qx) * np_
            for half in range(2):
                places = [tap_of(taps, r, s, qy, qx) for s in (2 * half, 2 * half + 1) for r in range(4)]
                value = choose(places, 16, cout)
                wt[n : n + cout, offset + half * 128 : offset + half * 128 + 128] = value.astype(BF)


SUMS = {(0, 0): (0, 1), (0, 1): (2,), (1, 0): (0,), (1, 1): (1, 2)}


def prepare_up(wt, w, number, count, lanes):
    cout, np_ = COUT[number], NP[number]
    if lanes == 128:
        taps = [[w[ky, kx][:, :count].astype(F32) for kx in range(3)] for ky in range(3)]
    else:
        taps = replicated_taps(w, number, 0, count, lanes)
    for qy in range(2):
        for t in range(2):
            for qx in range(2):
                n = (qy * 2 + qx) * np_
                parts = []
                for u in range(2):
                    total = None
                    for ky in SUMS[qy, t]:
                        for kx in SUMS[qx, u]:
                            total = taps[ky][kx] if total is None else total + taps[ky][kx]
                    parts.append(total)
                if lanes == 128:
                    for u in range(2):
                        k = (t * 2 + u) * 128
                        wt[n : n + cout, k : k + count] = parts[u].astype(BF)
                else:
                    wt[n : n + cout, t * 128 : t * 128 + 128] = choose(parts, lanes, cout).astype(BF)


def kernel(sizes, feat, *refs):
    rows_ty, cols_tx = sizes
    weights = refs[:16]
    table = refs[16]
    out = refs[17]
    c = dict(zip(SCRATCH, refs[18 : 18 + len(SCRATCH)]))
    send1, recv1, send2, recv2 = refs[18 + len(SCRATCH) :]
    ty = lax.axis_index("ty")
    tx = lax.axis_index("tx")

    def device(dy, dx):
        return (lax.rem(ty + dy + rows_ty, rows_ty), lax.rem(tx + dx + cols_tx, cols_tx))

    barrier = pltpu.get_barrier_semaphore()
    for dy, dx in FAR:
        pl.semaphore_signal(barrier, inc=1, device_id=device(dy, dx), device_id_type=MESH)

    lane9 = iota((9, 8, 128), 2)
    for side in range(2):
        value = jnp.zeros((9, 8, 128), F32)
        for g in range(4):
            piece = feat[:, 8 * g : 8 * g + 8, 128 * side : 128 * side + 128].astype(F32)
            shift = (32 * g - 96 * side) % 128
            if shift:
                piece = pltpu.roll(piece, shift, 2)
            value = jnp.where((lane9 >= 32 * g) & (lane9 < 32 * g + 32), piece, value)
        c["cols_out"][side, 0:72, :] = value.reshape(72, 128).astype(BF)
        c["cols_out"][side, 64:80, :] = jnp.concatenate(
            [value.reshape(72, 128)[64:72], jnp.zeros((8, 128), F32)], 0
        ).astype(BF)

    pl.semaphore_wait(barrier, len(FAR))
    copies = []
    for number, (dy, dx) in enumerate(DIRS):
        if dx == 0:
            source, target = feat, c["rows_in"].at[0 if dy == 1 else 1]
        else:
            source = c["cols_out"].at[0 if dx == -1 else 1]
            target = c["cols_in"].at[(0 if dx == -1 else 3) + dy + 1]
        copy = pltpu.make_async_remote_copy(
            src_ref=source,
            dst_ref=target,
            send_sem=send1.at[number],
            recv_sem=recv1.at[number],
            device_id=device(dy, dx),
            device_id_type=MESH,
        )
        copy.start()
        copies.append(copy)

    for number in (2, 4, 5, 6, 7, 8, 9, 10):
        c["w%d" % number][...] = jnp.zeros(c["w%d" % number].shape, BF)
    prepare_window(c["w0"], weights[0], 0, 0, 0)
    prepare_blocks(c["w1"], weights[1], 1, 0, 0, 32, 32)
    prepare_blocks(c["w2"], weights[2], 2, 0, 0, 32, 32)
    prepare_blocks(c["w3"], weights[3], 3, 0, 0, 48, 64)

    place = iota((384, 1024), 0)
    target = iota((384, 1024), 1)
    x = jnp.where(place < 256, place, jnp.where(place < 288, place - 288, jnp.where(place < 320, place - 32, -1000)))
    want = 2 * (target % 256) + target // 256 - 36
    c["spread"][...] = (x == want).astype(F32).astype(BF)
    c["eye"][...] = (iota((160, 256), 0) == iota((160, 256), 1)).astype(F32).astype(BF)
    for k in range(8):
        c["planar"][k, 864:1536, :] = jnp.zeros((672, 128), F32)

    for copy in copies:
        copy.wait()

    first_row = jnp.where(ty > 0, 1.0, 0.0)
    last_row = jnp.where(ty < rows_ty - 1, 1.0, 0.0)
    first_col = jnp.where(tx > 0, 1.0, 0.0)
    last_col = jnp.where(tx < cols_tx - 1, 1.0, 0.0)
    c["ext"][:, 0:32, 0:256] = jnp.where(first_row > 0, c["rows_in"][0].astype(F32), 0.0).astype(BF)
    c["ext"][:, 32:64, 0:256] = feat[...]
    c["ext"][:, 64:96, 0:256] = jnp.where(last_row > 0, c["rows_in"][1].astype(F32), 0.0).astype(BF)
    for k in range(3):
        row_ok = (first_row, 1.0, last_row)[k]
        left = c["cols_in"][3 + (1, 0, -1)[k] + 1].astype(F32)[0:72].reshape(9, 8, 128)
        right = c["cols_in"][(1, 0, -1)[k] + 1].astype(F32)[0:72].reshape(9, 8, 128)
        left = jnp.where(row_ok * first_col > 0, left, 0.0)
        right = jnp.where(row_ok * last_col > 0, right, 0.0)
        for g in range(4):
            to_left = pltpu.roll(left, (128 - 32 * g) % 128, 2) if g else left
            to_right = pltpu.roll(right, (160 - 32 * g) % 128, 2) if g != 1 else right
            piece = jnp.where(lane9 < 32, to_left, jnp.where(lane9 < 64, to_right, 0.0))
            c["ext_side"][:, 32 * k + 8 * g : 32 * k + 8 * g + 8, :] = piece
    c["ext"][:, :, 256:384] = c["ext_side"][...].astype(BF)

    def spread_channel(ch, _):
        wide = jnp.dot(c["ext"][ch], c["spread"][...], preferred_element_type=F32)
        for k in range(8):
            c["planar"][k, pl.ds(pl.multiple_of(ch * 96, 96), 96), :] = wide[:, 128 * k : 128 * k + 128]
        return 0

    lax.fori_loop(0, 9, spread_channel, 0)

    def gather_row(y, _):
        for k in range(8):
            c["rows_yc"][y, :, 128 * k : 128 * k + 128] = c["planar"][k, pl.ds(y + 12, 16, stride=96), :].astype(BF)
        return 0

    lax.fori_loop(0, 72, gather_row, 0)

    def column_caps(number, wp, origin, width):
        np_ = NP[number]
        n = 4 * np_
        cap = c["cap%d" % n]
        at = origin + 2 * iota((wp, n), 0) + (iota((wp, n), 1) // np_) % 2 + tx * width
        cap[0:wp, :] = jnp.where((at >= 0) & (at < width * cols_tx), BIG, 0.0)
        return cap

    def finish(number, r, cap, i0, g, wp, origin, height):
        np_ = NP[number]
        n = 4 * np_
        u = jnp.maximum(r + table[number : number + 1, 0:n], 0.0)
        pieces = []
        for k in range(g):
            at = origin + 2 * (i0 + k) + iota((1, n), 1) // (2 * np_) + ty * height
            row = jnp.where((at >= 0) & (at < height * rows_ty), BIG, 0.0)
            pieces.append(jnp.minimum(u[k * wp : (k + 1) * wp], jnp.minimum(cap[0:wp, :], row)))
        return pieces

    def to_blocks(pieces, target, i0, wp, n):
        t = c["t%d" % n]
        g = len(pieces)
        for k in range(g):
            t[k * wp : (k + 1) * wp, :] = pieces[k]
            target[i0 + k, :, 0:n] = pieces[k].astype(BF)
        for k in range(g):
            target[i0 + k, :, n : 2 * n] = t[k * wp + 1 : (k + 1) * wp + 1, :].astype(BF)

    def pooled(piece, np_):
        if np_ == 32:
            m = jnp.maximum(piece, pltpu.roll(piece, 64, 1))
            return jnp.maximum(m, pltpu.roll(m, 32, 1))
        if np_ == 64:
            m = jnp.maximum(piece[:, 0:128], piece[:, 128:256])
            return jnp.maximum(m, pltpu.roll(m, 64, 1))
        m = jnp.maximum(piece[:, 0:128], piece[:, 128:256])
        return jnp.maximum(m, jnp.maximum(piece[:, 256:384], piece[:, 384:512]))

    def pack(pixels, target, count, wp, lanes, row0, col0):
        lane = iota((wp, 128), 1)

        def step(i, _):
            a = [
                [pixels[row0 + 2 * i + py, pl.ds(col0 + m, wp, stride=2), :] for m in range(4)] for py in range(2)
            ]
            for u in range(2):
                four = [a[0][2 * u], a[0][2 * u + 1], a[1][2 * u], a[1][2 * u + 1]]
                base = u * 4 * lanes
                if lanes == 32:
                    v = jnp.where(
                        lane < 64,
                        jnp.where(lane < 32, four[0], four[1]),
                        jnp.where(lane < 96, four[2], four[3]),
                    )
                    target[i, :, base : base + 128] = v.astype(BF)
                elif lanes == 64:
                    for py in range(2):
                        v = jnp.where(lane < 64, four[2 * py], four[2 * py + 1])
                        target[i, :, base + 128 * py : base + 128 * py + 128] = v.astype(BF)
                else:
                    for q in range(4):
                        target[i, :, base + 128 * q : base + 128 * q + 128] = four[q].astype(BF)
            return 0

        lax.fori_loop(0, count, step, 0)

    def to_pixels(pieces, target, i0, wp, wr, np_):
        td = c["td"]
        lane = iota((wp, 128), 1)
        lane_r = iota((wr, 128), 1)
        for k in range(len(pieces)):
            for qy in range(2):
                at = 2 * k + qy
                if np_ == 128:
                    even = pieces[k][:, 256 * qy : 256 * qy + 128]
                    odd = pieces[k][:, 256 * qy + 128 : 256 * qy + 256]
                else:
                    v = pieces[k][:, 128 * qy : 128 * qy + 128]
                    w = pltpu.roll(v, 64, 1)
                    even = jnp.where(lane < 64, v, w)
                    odd = jnp.where(lane < 64, w, v)
                td[at, pl.ds(0, wp, stride=2), :] = even
                td[at, pl.ds(1, wp, stride=2), :] = odd
        for k in range(len(pieces)):
            for qy in range(2):
                at = 2 * k + qy
                here, right = td[at, 0:wr, :], td[at, 1 : wr + 1, :]
                if np_ == 128:
                    target[2 * (i0 + k) + qy, :, 0:128] = here.astype(BF)
                    target[2 * (i0 + k) + qy, :, 128:256] = right.astype(BF)
                else:
                    target[2 * (i0 + k) + qy, :, :] = jnp.where(lane_r < 64, here, right).astype(BF)

    def block_input(ref):
        def load(i0, g):
            lanes = ref.shape[2]
            rows = g * ref.shape[1]
            return [
                ref[pl.ds(i0, g)].reshape(rows, lanes),
                ref[pl.ds(i0 + 1, g)].reshape(rows, lanes),
            ]

        return load

    def layer(number, loads, count, g, wp, origin_y, origin_x, level, store):
        height, width = 32 >> level, 256 >> level
        cap = column_caps(number, wp, origin_x, width)

        def step(it, _):
            i0 = it * g
            lhs = []
            for load in loads:
                lhs = lhs + load(i0, g)
            lhs = jnp.concatenate(lhs, axis=1) if len(lhs) > 1 else lhs[0]
            r = nt(lhs, c["w%d" % number][...])
            store(finish(number, r, cap, i0, g, wp, origin_y, height), i0)
            return 0

        if count == 1:
            step(0, 0)
        else:
            lax.fori_loop(0, count, step, 0)

    def pool_into(pixels, number, wp):
        def store(pieces, i0):
            for k, piece in enumerate(pieces):
                pixels[i0 + k, 0:wp, :] = pooled(piece, NP[number])

        return store

    def windows(i, _):
        rows = c["rows_yc"][pl.ds(2 * i, 4)].reshape(64, 1024)
        stacked = jnp.concatenate([rows[:, 256 * s : 256 * s + 256] for s in range(4)], axis=0)
        c["fwin"][i] = nt(c["eye"][...], stacked).astype(BF)
        return 0

    lax.fori_loop(0, 35, windows, 0)

    def window_load(i0, g):
        return [c["fwin"][pl.ds(i0, g)].reshape(g * 160, 256)]

    layer(0, [window_load], 7, 5, 160, -19, -35, 0, lambda p, i0: to_blocks(p, c["s1"], i0, 160, 128))
    layer(1, [block_input(c["s1"])], 17, 2, 160, -18, -34, 0, pool_into(c["pix1"], 1, 160))
    pack(c["pix1"], c["s2"], 17, 80, 32, 0, 8)
    layer(2, [block_input(c["s2"])], 4, 4, 80, -8, -8, 1, pool_into(c["pix2"], 2, 80))
    pack(c["pix2"], c["s3"], 5, 48, 64, 3, 3)
    layer(3, [block_input(c["s3"])], 1, 4, 48, 0, 0, 2, pool_into(c["pix3o"], 3, 48))

    lane16 = iota((16, 128), 1)
    for y in range(4):
        even = c["pix3o"][y, pl.ds(0, 16, stride=2), :]
        odd = c["pix3o"][y, pl.ds(1, 16, stride=2), :]
        c["tile_out"][16 * y : 16 * y + 16, :] = jnp.where(lane16 < 64, even, odd).astype(BF)
    copies = []
    for number, (dy, dx) in enumerate(FAR):
        copy = pltpu.make_async_remote_copy(
            src_ref=c["tile_out"],
            dst_ref=c["tiles_in"].at[number],
            send_sem=send2.at[number],
            recv_sem=recv2.at[number],
            device_id=device(dy, dx),
            device_id_type=MESH,
        )
        copy.start()
        copies.append(copy)

    prepare_blocks(c["w4"], weights[4], 4, 0, 0, 64, 64)
    prepare_blocks(c["w5"], weights[5], 5, 0, 0, 80, 128)
    prepare_blocks(c["w6"], weights[6], 6, 0, 0, 96, 128)
    prepare_up(c["w7"], weights[7], 7, 96, 128)
    prepare_blocks(c["w7"], weights[7], 7, 512, 96, 64, 64)
    prepare_blocks(c["w8"], weights[8], 8, 0, 0, 112, 128)
    prepare_up(c["w9"], weights[9], 9, 112, 128)
    prepare_blocks(c["w9"], weights[9], 9, 512, 112, 48, 64)
    prepare_blocks(c["w10"], weights[10], 10, 0, 0, 96, 128)
    prepare_blocks(c["w12"], weights[12], 12, 0, 0, 64, 64)
    prepare_up(c["w13"], weights[13], 13, 64, 64)
    prepare_window(c["w13"], weights[13], 13, 256, 64)
    prepare_blocks(c["w14"], weights[14], 14, 0, 0, 64, 64)
    c["w11"][...] = jnp.zeros(c["w11"].shape, BF)
    prepare_up(c["w11"], weights[11], 11, 96, 128)
    prepare_blocks(c["w11"], weights[11], 11, 512, 96, 32, 32)
    taps = replicated_taps(weights[15], 15, 0, 32, 32)
    c["w15f"][...] = jnp.zeros((16, 512), F32)
    for qx in range(2):
        for qy in range(2):
            n = qx * 8 + qy * 3
            for t in range(2):
                for u in range(2):
                    places = [tap_of(taps, 2 * t + py, 2 * u + px, qy, qx) for py in range(2) for px in range(2)]
                    k = (t * 2 + u) * 128
                    c["w15f"][n : n + 3, k : k + 128] = choose(places, 32, 3)
    c["w15"][...] = c["w15f"][...].astype(BF)
    pack(c["pix1"], c["k11"], 12, 80, 32, 5, 13)
    pack(c["pix2"], c["k9"], 8, 48, 64, 0, 0)

    for copy in copies:
        copy.wait()

    slot = {d: n for n, d in enumerate(FAR)}
    for ky in range(-3, 4):
        for kx in range(-1, 2):
            if (ky, kx) == (0, 0):
                tile = c["tile_out"][...].astype(F32)
            else:
                ok = (ty + ky >= 0) & (ty + ky < rows_ty) & (tx + kx >= 0) & (tx + kx < cols_tx)
                tile = jnp.where(jnp.where(ok, 1.0, 0.0) > 0, c["tiles_in"][slot[-ky, -kx]].astype(F32), 0.0)
            for y in range(4):
                if ky == -3 and y < 3 or ky == 3 and y > 0:
                    continue
                v = tile[16 * y : 16 * y + 16]
                w = pltpu.roll(v, 64, 1)
                row = 12 + 4 * ky + y
                col = 32 * (kx + 1)
                c["pix3"][row, pl.ds(col, 16, stride=2), :] = jnp.where(lane16 < 64, v, w)
                c["pix3"][row, pl.ds(col + 1, 16, stride=2), :] = jnp.where(lane16 < 64, w, v)

    pack(c["pix3"], c["s4"], 11, 32, 64, 3, 23)
    pack(c["pix3"], c["k7"], 6, 32, 64, 8, 28)

    layer(4, [block_input(c["s4"])], 2, 5, 32, -8, -8, 3, pool_into(c["pix4"], 4, 32))
    pack(c["pix4"], c["s5"], 5, 16, 128, 0, 0)
    layer(5, [block_input(c["s5"])], 1, 4, 16, -3, -3, 4, lambda p, i0: to_blocks(p, c["s6"], i0, 16, 512))
    layer(6, [block_input(c["s6"])], 1, 3, 16, -2, -2, 4, lambda p, i0: to_pixels(p, c["r7"], i0, 16, 32, 128))
    layer(
        7, [block_input(c["r7"]), block_input(c["k7"])], 1, 5, 32, -3, -3, 3,
        lambda p, i0: to_blocks(p, c["s8"], i0, 32, 512),
    )
    layer(8, [block_input(c["s8"])], 1, 4, 32, -2, -2, 3, lambda p, i0: to_pixels(p, c["r9"], i0, 32, 48, 128))
    layer(
        9, [block_input(c["r9"]), block_input(c["k9"])], 1, 7, 48, -3, -3, 2,
        lambda p, i0: to_blocks(p, c["s10"], i0, 48, 512),
    )
    layer(10, [block_input(c["s10"])], 1, 6, 48, -2, -2, 2, lambda p, i0: to_pixels(p, c["r11"], i0, 48, 80, 128))
    layer(
        11, [block_input(c["r11"]), block_input(c["k11"])], 1, 11, 80, -3, -3, 1,
        lambda p, i0: to_blocks(p, c["s12"], i0, 80, 256),
    )
    layer(12, [block_input(c["s12"])], 2, 5, 80, -2, -2, 1, lambda p, i0: to_pixels(p, c["r13"], i0, 80, 144, 64))

    def features_load(i0, g):
        return [c["fwin"][pl.ds(i0 + 8, g), 16:160, :].reshape(g * 144, 256)]

    layer(
        13, [block_input(c["r13"]), features_load], 5, 4, 144, -3, -3, 0,
        lambda p, i0: to_blocks(p, c["s14"], i0, 144, 256),
    )
    layer(14, [block_input(c["s14"])], 6, 3, 144, -2, -2, 0, lambda p, i0: to_blocks(p, c["s15"], i0, 144, 128))

    lane144 = iota((16, 144), 1)

    def last(i, _):
        field = jnp.concatenate([c["s15"][i], c["s15"][i + 1]], axis=1)
        r = nt(c["w15"][...], field) + table[16:32, 0:144]
        r = jnp.where(lane144 < 129, r, 0.0)
        c["z0"][pl.ds(pl.multiple_of(8 * i, 8), 8), :] = r[0:8]
        c["z1"][pl.ds(pl.multiple_of(8 * i, 8), 8), :] = r[8:16]
        return 0

    c["z0"][136:144, :] = jnp.zeros((8, 144), F32)
    c["z1"][136:144, :] = jnp.zeros((8, 144), F32)
    lax.fori_loop(0, 17, last, 0)
    at = iota((144, 256), 1) - 2 * iota((144, 256), 0)
    even = (at == -1).astype(F32).astype(BF)
    odd = (at == 0).astype(F32).astype(BF)
    wide = jnp.dot(c["z0"][...].astype(BF), even, preferred_element_type=F32) + jnp.dot(
        c["z1"][...].astype(BF), odd, preferred_element_type=F32
    )
    for half in range(2):
        lanes = slice(128 * half, 128 * half + 128)
        c["zf"][half] = wide[:, lanes]
        for o in range(3):
            c["out32"][2 * o + half, pl.ds(0, 16, stride=2), :] = c["zf"][half, pl.ds(3 + o, 16, stride=8), :]
            c["out32"][2 * o + half, pl.ds(1, 16, stride=2), :] = c["zf"][half, pl.ds(8 + o, 16, stride=8), :]
            out[o, :, lanes] = c["out32"][2 * o + half].astype(BF)


def bias_table(biases):
    rows = []
    offset = 0
    for number in range(16):
        piece = biases[offset : offset + COUT[number]]
        offset = offset + COUT[number]
        if number == 15:
            six = jnp.concatenate([piece, piece, jnp.zeros((2,), F32)])
            column = jnp.concatenate([six, six])
            rows.append(jnp.zeros((1, 512), F32))
            rows.append(jnp.broadcast_to(column[:, None], (16, 512)))
        else:
            phase = jnp.pad(piece, (0, NP[number] - COUT[number]))
            four = jnp.concatenate([phase] * 4)
            rows.append(jnp.pad(four, (0, 512 - 4 * NP[number]))[None])
    return jnp.concatenate(rows, axis=0)


def body(sizes, features, *rest):
    weights, biases = rest[:16], rest[16]
    vmem = pl.BlockSpec(memory_space=pltpu.VMEM)
    scratch = [pltpu.VMEM(shape, kind) for shape, kind in SCRATCH.values()]
    scratch += [pltpu.SemaphoreType.DMA((n,)) for n in (8, 8, 20, 20)]
    return pl.pallas_call(
        functools.partial(kernel, sizes),
        out_shape=jax.ShapeDtypeStruct((3, 32, 256), BF),
        in_specs=[vmem] * 18,
        out_specs=vmem,
        scratch_shapes=scratch,
        compiler_params=pltpu.CompilerParams(
            collective_id=0, has_side_effects=True, vmem_limit_bytes=58 << 20
        ),
    )(features, *weights, bias_table(biases))


def solution(mesh):
    sizes = (mesh.shape["ty"], mesh.shape["tx"])
    return jax.shard_map(
        functools.partial(body, sizes),
        mesh=mesh,
        in_specs=(P(None, "ty", "tx"),) + (P(),) * 17,
        out_specs=P(None, "ty", "tx"),
        check_vma=False,
    )
```

time: 397 us -> 84.9 us (0.21)
  the two profiles are of different devices: /device:TPU:111 before, /device:TPU:1 now
where the time goes in v1:
time: 84.9 us; the launch traced here: 84.6 us
  Pallas kernels  71.9 us (85%)
  local copies, waits for them, and re-layouts  12.2 us (14%)
    pallas_call x1, Pallas kernels, body(): pl.pallas_call(functools.partial(kernel, sizes), out_shape=jax.ShapeDtype...  71.9 us
    unnamed x24, local copies, waits for them, and re-layouts  7.46 us
    slice x7, local copies, waits for them, and re-layouts, bias_table(): piece = biases[offset:offset + COUT[number]]  2.64 us
    concatenate x1, local copies, waits for them, and re-layouts, bias_table(): return jnp.concatenate(rows, axis=0)  1.88 us

profile of v1, /device:TPU:1, one launch (start us, length us, event | category | flops | bytes accessed | tf_op | source)
XLA Modules:
  0.0 84.6 jit_solution(16240604817968596114)
XLA Ops:
  0.0 0.0 copy-start.7
  0.0 0.8 slice.52
  0.8 0.8 slice.50
  1.6 0.8 slice.63
  2.4 0.1 concatenate.68
  2.4 0.0 copy-done.7
  2.4 0.1 fusion.3
  2.6 0.1 select_maximum_fusion.15
  2.6 0.1 fusion
  2.7 0.1 select_maximum_fusion.21
  2.8 0.1 fusion.2
  3.0 0.1 fusion.1
  3.0 0.1 select_maximum_fusion.3
  3.1 0.1 select_maximum_fusion
  3.2 0.1 select_maximum_fusion.9
  3.3 0.1 broadcast_in_dim.70
  3.3 0.0 copy-start.6
  3.3 0.0 copy-start.5
  3.4 1.9 %concatenate.69.refs_16_ = f32[32,512]{1,0:T(8,128)} concatenate(f32[1,512]{1,0:T(1,128)S(1)} %bitcast.19, f32[1,512]{1,0:T(1,128)S(1)} %bitcast.27, f32[1,512]{1,0:T(1,128)S(1)} %bitcast.17, f32[1,512]{1,0:T(1,128)S(1)} %bitcast.29, f32[1,512]{1,0:T(1,128)S(1)} %bitcast.18, f32[1,512]{1,0:T(1,128)S(1)} %bitcast.20, f32[1,512]{1,0:T(1,128)S(1)} %bitcast.21, ...), dimensions={0} | concatenate | bytes 131072 | tf_op jit(solution)/shard_map/concatenate | solution.py:573
  5.2 0.0 copy-done.6
  5.2 0.0 copy-start.4
  5.2 0.8 copy.19.refs_0_
  6.0 0.0 copy-done.5
  6.0 0.0 copy-start.3
  6.0 0.8 copy.20.refs_2_
  6.8 0.0 copy-done.4
  6.8 0.0 copy-start.2
  6.8 0.8 copy.21.refs_3_
  7.6 0.0 copy-done.3
  7.6 0.0 copy-start.1
  7.6 0.8 copy.22.refs_4_
  8.4 0.0 copy-done.2
  8.4 0.8 %copy.23.refs_5_ = bf16[3,3,96,80]{3,2,1,0:T(8,128)(2,1)} copy(bf16[3,3,96,80]{2,3,1,0:T(8,128)(2,1)S(1)} %copy-done.2) | data formatting | bytes 276480 | tf_op args[6]
  9.2 0.0 copy-done.1
  9.2 0.0 copy-start
  9.2 1.0 %copy.25.refs_9_ = bf16[3,3,96,160]{3,2,1,0:T(8,128)(2,1)} copy(bf16[3,3,96,160]{2,3,1,0:T(8,128)(2,1)S(1)} %copy-done.1) | data formatting | bytes 552960 | tf_op args[10]
  10.2 0.0 copy-done
  10.2 1.0 %copy.24.refs_7_ = bf16[3,3,112,160]{3,2,1,0:T(8,128)(2,1)} copy(bf16[3,3,112,160]{2,3,1,0:T(8,128)(2,1)S(1)} %copy-done) | data formatting | bytes 645120 | tf_op args[8]
  11.3 71.9 %shard_map.172 = bf16[3,32,256]{2,1,0:T(8,128)(2,1)} custom-call(bf16[9,32,256]{2,1,0:T(8,128)(2,1)} %feat.1, bf16[3,3,32,9]{3,2,1,0:T(8,128)(2,1)} %copy.19.refs_0_, bf16[3,3,32,32]{3,2,1,0:T(8,128)(2,1)} %refs_1_.1, bf16[3,3,48,32]{3,2,1,0:T(8,128)(2,1)} %copy.20.refs_2_, bf16[3,3,64,48]{3,2,1,0:T(8,128)(2,1)} %copy.21.refs_3_, ...), custom_call_target="tpu_custom_call" | custom-call | tf_op jit(solution)/shard_map/pallas_call | solution.py:581
  83.1 1.4 %copy.27 = bf16[3,32,256]{2,1,0:T(8,128)(2,1)} copy(bf16[3,32,256]{2,1,0:T(8,128)(2,1)} %shard_map.172) | data formatting | bytes 98304
  (17 shorter events, 0.1 us)
Async XLA Ops:
  0.0 2.4 %copy-start.7 = (f32[1091]{0:T(1024)S(1)}, f32[1091]{0:T(1024)}, u32[]{:S(2)}) copy-start(f32[1091]{0:T(1024)} %param.35) | copy-start | bytes 13096
  3.3 1.9 %copy-start.6 = (bf16[3,3,32,9]{2,1,3,0:T(4,128)(2,1)S(1)}, bf16[3,3,32,9]{2,1,3,0:T(4,128)(2,1)}, u32[]{:S(2)}) copy-start(bf16[3,3,32,9]{2,1,3,0:T(4,128)(2,1)} %param.19) | copy-start | bytes 15556
  3.3 2.7 %copy-start.5 = (bf16[3,3,48,32]{2,3,1,0:T(8,128)(2,1)S(1)}, bf16[3,3,48,32]{2,3,1,0:T(8,128)(2,1)}, u32[]{:S(2)}) copy-start(bf16[3,3,48,32]{2,3,1,0:T(8,128)(2,1)} %param.21) | copy-start | bytes 82948
  5.2 1.5 %copy-start.4 = (bf16[3,3,64,48]{2,3,1,0:T(8,128)(2,1)S(1)}, bf16[3,3,64,48]{2,3,1,0:T(8,128)(2,1)}, u32[]{:S(2)}) copy-start(bf16[3,3,64,48]{2,3,1,0:T(8,128)(2,1)} %param.22) | copy-start | bytes 165892
  6.0 1.6 %copy-start.3 = (bf16[3,3,80,64]{2,3,1,0:T(8,128)(2,1)S(1)}, bf16[3,3,80,64]{2,3,1,0:T(8,128)(2,1)}, u32[]{:S(2)}) copy-start(bf16[3,3,80,64]{2,3,1,0:T(8,128)(2,1)} %param.23) | copy-start | bytes 276484
  6.8 1.6 %copy-start.2 = (bf16[3,3,96,80]{2,3,1,0:T(8,128)(2,1)S(1)}, bf16[3,3,96,80]{2,3,1,0:T(8,128)(2,1)}, u32[]{:S(2)}) copy-start(bf16[3,3,96,80]{2,3,1,0:T(8,128)(2,1)} %param.24) | copy-start | bytes 414724
  7.6 1.7 %copy-start.1 = (bf16[3,3,96,160]{2,3,1,0:T(8,128)(2,1)S(1)}, bf16[3,3,96,160]{2,3,1,0:T(8,128)(2,1)}, u32[]{:S(2)}) copy-start(bf16[3,3,96,160]{2,3,1,0:T(8,128)(2,1)} %param.28) | copy-start | bytes 829444
  9.2 1.0 %copy-start = (bf16[3,3,112,160]{2,3,1,0:T(8,128)(2,1)S(1)}, bf16[3,3,112,160]{2,3,1,0:T(8,128)(2,1)}, u32[]{:S(2)}) copy-start(bf16[3,3,112,160]{2,3,1,0:T(8,128)(2,1)} %param.26) | copy-start | bytes 967684

commit v2 on v1

--- a/solution.py
+++ b/solution.py
@@ -27,9 +27,9 @@
     tiles_in=((20, 64, 128), BF),
     ext_side=((9, 96, 128), F32),
     ext=((9, 96, 384), BF),
-    spread=((384, 1024), BF),
-    planar=((8, 16 * 96, 128), F32),
-    rows_yc=((72, 16, 1024), BF),
+    spread=((384, 512), BF),
+    planar=((4, 16 * 96, 128), F32),
+    rows_yc=((72, 16, 512), BF),
     eye=((160, 256), BF),
     fwin=((40, 160, 256), BF),
     s1=((36, 160, 256), BF),
@@ -55,21 +55,25 @@
     r13=((24, 144, 128), BF),
     s14=((21, 144, 512), BF),
     s15=((20, 144, 256), BF),
-    t128=((968, 128), F32),
-    t256=((968, 256), F32),
+    t128=((1928, 128), F32),
+    t256=((1448, 256), F32),
     t512=((360, 512), F32),
     td=((20, 184, 128), F32),
     cap128=((160, 128), F32),
     cap256=((144, 256), F32),
     cap512=((48, 512), F32),
     w15f=((16, 512), F32),
+    flat=((16, 128), F32),
+    table=((16, 512), F32),
+    column=((16, 144), F32),
     z0=((144, 144), F32),
     z1=((144, 144), F32),
     zf=((2, 144, 128), F32),
     out32=((6, 32, 128), F32),
 )
 for _k in range(16):
-    SCRATCH["w%d" % _k] = ((16 if _k == 15 else 4 * NP[_k], KDIM[_k]), BF)
+    _n = 16 if _k == 15 else 4 * NP[_k]
+    SCRATCH["w%d" % _k] = ((KDIM[_k], _n) if _k in (0, 2, 3, 4, 5, 7, 9) else (_n, KDIM[_k]), BF)
 
 
 def iota(shape, dim):
@@ -80,107 +84,97 @@
     return lax.dot_general(a, b, (((1,), (1,)), ((), ())), preferred_element_type=F32)
 
 
-def replicated_taps(w, number, first, count, period):
-    cin = CIN[number]
-    row = iota((cin, 128), 0)
-    lane = iota((cin, 128), 1)
-    pick = ((row - first == lane % period) & (row >= first) & (row < first + count)).astype(F32).astype(BF)
-    return [
-        [jnp.dot(w[ky, kx], pick, preferred_element_type=F32) for kx in range(3)] for ky in range(3)
-    ]
-
-
-def choose(groups, period, rows):
-    lane = iota((rows, 128), 1)
-    value = jnp.zeros((rows, 128), F32)
-    for place, tap in enumerate(groups):
-        if tap is not None:
-            value = jnp.where((lane >= place * period) & (lane < (place + 1) * period), tap, value)
-    return value
-
-
-def tap_of(taps, r, s, qy, qx):
-    ky, kx = r - qy, s - qx
-    if 0 <= ky < 3 and 0 <= kx < 3:
-        return taps[ky][kx]
-    return None
+FLIPPED = (0, 2, 3, 4, 5, 7, 9)
+
+
+def tap_of(w, number, ky, kx, first, count):
+    if number == 0:
+        return w[ky, :, kx, :]
+    if number in FLIPPED:
+        return w[ky, kx, first : first + count, :]
+    return w[ky, kx][:, first : first + count]
+
+
+def put(wt, number, n, k, tap):
+    if number in FLIPPED:
+        wt[k : k + tap.shape[0], n : n + tap.shape[1]] = tap
+    else:
+        wt[n : n + tap.shape[0], k : k + tap.shape[1]] = tap
 
 
 def prepare_blocks(wt, w, number, offset, first, count, lanes):
-    cout, np_ = COUT[number], NP[number]
-    if lanes == 128:
-        for ky in range(3):
-            for kx in range(3):
-                tap = w[ky, kx]
-                for qy in range(2):
-                    for qx in range(2):
-                        r, s = ky + qy, kx + qx
-                        t, py, u, px = r // 2, r % 2, s // 2, s % 2
-                        k = offset + ((t * 2 + u) * 4 + py * 2 + px) * 128
-                        n = (qy * 2 + qx) * np_
-                        wt[n : n + cout, k : k + count] = tap
-        return
-    taps = replicated_taps(w, number, first, count, lanes)
-    per = 128 // lanes
-    for qy in range(2):
-        for qx in range(2):
-            n = (qy * 2 + qx) * np_
-            for t in range(2):
-                for u in range(2):
-                    places = [tap_of(taps, 2 * t + py, 2 * u + px, qy, qx) for py in range(2) for px in range(2)]
-                    for chunk in range(4 // per):
-                        k = offset + (t * 2 + u) * 4 * lanes + chunk * 128
-                        value = choose(places[chunk * per : (chunk + 1) * per], lanes, cout)
-                        wt[n : n + cout, k : k + 128] = value.astype(BF)
+    for ky in range(3):
+        for kx in range(3):
+            tap = tap_of(w, number, ky, kx, first, count)
+            for qy in range(2):
+                for qx in range(2):
+                    r, s = ky + qy, kx + qx
+                    k = offset + ((r // 2 * 2 + s // 2) * 4 + r % 2 * 2 + s % 2) * lanes
+                    put(wt, number, (qy * 2 + qx) * NP[number], k, tap)
 
 
 def prepare_window(wt, w, number, offset, first):
-    cout, np_ = COUT[number], NP[number]
-    taps = replicated_taps(w, number, first, 9, 16)
-    for qy in range(2):
-        for qx in range(2):
-            n = (qy * 2 + qx) * np_
-            for half in range(2):
-                places = [tap_of(taps, r, s, qy, qx) for s in (2 * half, 2 * half + 1) for r in range(4)]
-                value = choose(places, 16, cout)
-                wt[n : n + cout, offset + half * 128 : offset + half * 128 + 128] = value.astype(BF)
+    for ky in range(3):
+        for kx in range(3):
+            tap = tap_of(w, number, ky, kx, first, 9)
+            for qy in range(2):
+                for qx in range(2):
+                    k = offset + (kx + qx) * 64 + (ky + qy) * 16
+                    put(wt, number, (qy * 2 + qx) * NP[number], k, tap)
 
 
 SUMS = {(0, 0): (0, 1), (0, 1): (2,), (1, 0): (0,), (1, 1): (1, 2)}
 
 
 def prepare_up(wt, w, number, count, lanes):
-    cout, np_ = COUT[number], NP[number]
-    if lanes == 128:
-        taps = [[w[ky, kx][:, :count].astype(F32) for kx in range(3)] for ky in range(3)]
-    else:
-        taps = replicated_taps(w, number, 0, count, lanes)
+    taps = [[tap_of(w, number, ky, kx, 0, count).astype(F32) for kx in range(3)] for ky in range(3)]
     for qy in range(2):
         for t in range(2):
+            rows = SUMS[qy, t]
+            line = taps[rows[0]] if len(rows) == 1 else [taps[rows[0]][kx] + taps[rows[1]][kx] for kx in range(3)]
             for qx in range(2):
-                n = (qy * 2 + qx) * np_
-                parts = []
                 for u in range(2):
-                    total = None
-                    for ky in SUMS[qy, t]:
-                        for kx in SUMS[qx, u]:
-                            total = taps[ky][kx] if total is None else total + taps[ky][kx]
-                    parts.append(total)
-                if lanes == 128:
-                    for u in range(2):
-                        k = (t * 2 + u) * 128
-                        wt[n : n + cout, k : k + count] = parts[u].astype(BF)
-                else:
-                    wt[n : n + cout, t * 128 : t * 128 + 128] = choose(parts, lanes, cout).astype(BF)
+                    cols = SUMS[qx, u]
+                    total = line[cols[0]] if len(cols) == 1 else line[cols[0]] + line[cols[1]]
+                    put(wt, number, (qy * 2 + qx) * NP[number], (t * 2 + u) * lanes, total.astype(BF))
+
+
+def prepare_biases(biases, flat, table, column):
+    flat[...] = jnp.zeros(flat.shape, F32)
+    for r in range(8):
+        flat[r : r + 1, :] = biases[pl.ds(128 * r, 128)].reshape(1, 128)
+    flat[8:9, 0:67] = biases[pl.ds(1024, 67)].reshape(1, 67)
+    lane = iota((8, 128), 1)
+    offset = 0
+    for number in range(16):
+        r, m = offset // 128, offset % 128
+        offset = offset + COUT[number]
+        pair = jnp.concatenate([flat[r : r + 1, :], flat[r + 1 : r + 2, :]], axis=1)
+        pair = jnp.broadcast_to(pair, (8, 256))
+        if m:
+            pair = pltpu.roll(pair, 256 - m, 1)
+        value = jnp.where(lane < COUT[number], pair[:, 0:128], 0.0)
+        if number == 15:
+            row = iota((16, 128), 0) % 8
+            twice = jnp.concatenate([value, value], axis=0)
+            mine = jnp.where((iota((16, 128), 1) == row % 3) & (row < 6), twice, 0.0)
+            column[...] = jnp.broadcast_to(jnp.sum(mine, axis=1, keepdims=True), (16, 144))
+            continue
+        if NP[number] == 32:
+            value = value + pltpu.roll(value, 32, 1)
+        if NP[number] <= 64:
+            value = value + pltpu.roll(value, 64, 1)
+        for k in range(4 * NP[number] // 128):
+            table[number : number + 1, 128 * k : 128 * k + 128] = value[0:1]
 
 
 def kernel(sizes, feat, *refs):
     rows_ty, cols_tx = sizes
     weights = refs[:16]
-    table = refs[16]
     out = refs[17]
     c = dict(zip(SCRATCH, refs[18 : 18 + len(SCRATCH)]))
     send1, recv1, send2, recv2 = refs[18 + len(SCRATCH) :]
+    table = c["table"]
     ty = lax.axis_index("ty")
     tx = lax.axis_index("tx")
 
@@ -204,6 +198,28 @@
         c["cols_out"][side, 64:80, :] = jnp.concatenate(
             [value.reshape(72, 128)[64:72], jnp.zeros((8, 128), F32)], 0
         ).astype(BF)
+
+    def clear(number):
+        c["w%d" % number][...] = jnp.zeros(c["w%d" % number].shape, BF)
+
+    for number in range(4):
+        clear(number)
+    prepare_window(c["w0"], weights[0], 0, 0, 0)
+    prepare_blocks(c["w1"], weights[1], 1, 0, 0, 32, 32)
+    prepare_blocks(c["w2"], weights[2], 2, 0, 0, 32, 32)
+    prepare_blocks(c["w3"], weights[3], 3, 0, 0, 48, 64)
+    prepare_biases(refs[16], c["flat"], c["table"], c["column"])
+
+    place = iota((384, 128), 0)
+    x = jnp.where(place < 256, place, jnp.where(place < 288, place - 288, jnp.where(place < 320, place - 32, -1000)))
+    x = x - 2 * iota((384, 128), 1) + 36
+    for px in range(2):
+        for half in range(2):
+            hit = jnp.where(x == px + 256 * half, 1.0, 0.0)
+            c["spread"][:, 256 * px + 128 * half : 256 * px + 128 * half + 128] = hit.astype(BF)
+    c["eye"][...] = (iota((160, 256), 0) == iota((160, 256), 1)).astype(F32).astype(BF)
+    for k in range(4):
+        c["planar"][k, 864:1536, :] = jnp.zeros((672, 128), F32)
 
     pl.semaphore_wait(barrier, len(FAR))
     copies = []
@@ -224,22 +240,34 @@
         copy.start()
         copies.append(copy)
 
-    for number in (2, 4, 5, 6, 7, 8, 9, 10):
-        c["w%d" % number][...] = jnp.zeros(c["w%d" % number].shape, BF)
-    prepare_window(c["w0"], weights[0], 0, 0, 0)
-    prepare_blocks(c["w1"], weights[1], 1, 0, 0, 32, 32)
-    prepare_blocks(c["w2"], weights[2], 2, 0, 0, 32, 32)
-    prepare_blocks(c["w3"], weights[3], 3, 0, 0, 48, 64)
-
-    place = iota((384, 1024), 0)
-    target = iota((384, 1024), 1)
-    x = jnp.where(place < 256, place, jnp.where(place < 288, place - 288, jnp.where(place < 320, place - 32, -1000)))
-    want = 2 * (target % 256) + target // 256 - 36
-    c["spread"][...] = (x == want).astype(F32).astype(BF)
-    c["eye"][...] = (iota((160, 256), 0) == iota((160, 256), 1)).astype(F32).astype(BF)
-    for k in range(8):
-        c["planar"][k, 864:1536, :] = jnp.zeros((672, 128), F32)
-
+    for number in range(4, 15):
+        clear(number)
+    prepare_blocks(c["w4"], weights[4], 4, 0, 0, 64, 64)
+    prepare_blocks(c["w5"], weights[5], 5, 0, 0, 80, 128)
+    prepare_blocks(c["w6"], weights[6], 6, 0, 0, 96, 128)
+    prepare_up(c["w7"], weights[7], 7, 96, 128)
+    prepare_blocks(c["w7"], weights[7], 7, 512, 96, 64, 64)
+    prepare_blocks(c["w8"], weights[8], 8, 0, 0, 112, 128)
+    prepare_up(c["w9"], weights[9], 9, 112, 128)
+    prepare_blocks(c["w9"], weights[9], 9, 512, 112, 48, 64)
+    prepare_blocks(c["w10"], weights[10], 10, 0, 0, 96, 128)
+    prepare_up(c["w11"], weights[11], 11, 96, 128)
+    prepare_blocks(c["w11"], weights[11], 11, 512, 96, 32, 32)
+    prepare_blocks(c["w12"], weights[12], 12, 0, 0, 64, 64)
+    prepare_up(c["w13"], weights[13], 13, 64, 64)
+    prepare_window(c["w13"], weights[13], 13, 256, 64)
+    prepare_blocks(c["w14"], weights[14], 14, 0, 0, 64, 64)
+    c["w15f"][...] = jnp.zeros((16, 512), F32)
+    for ky in range(3):
+        for kx in range(3):
+            tap = weights[15][ky, kx].astype(F32)
+            for qy in range(2):
+                for qx in range(2):
+                    r, s = ky + qy, kx + qx
+                    k = ((r // 2 * 2 + s // 2) * 4 + r % 2 * 2 + s % 2) * 32
+                    n = qx * 8 + qy * 3
+                    c["w15f"][n : n + 3, k : k + 32] = tap
+    c["w15"][...] = c["w15f"][...].astype(BF)
     for copy in copies:
         copy.wait()
 
@@ -265,18 +293,18 @@
 
     def spread_channel(ch, _):
         wide = jnp.dot(c["ext"][ch], c["spread"][...], preferred_element_type=F32)
-        for k in range(8):
+        for k in range(4):
             c["planar"][k, pl.ds(pl.multiple_of(ch * 96, 96), 96), :] = wide[:, 128 * k : 128 * k + 128]
         return 0
 
-    lax.fori_loop(0, 9, spread_channel, 0)
+    lax.fori_loop(0, 9, spread_channel, 0, unroll=3)
 
     def gather_row(y, _):
-        for k in range(8):
+        for k in range(4):
             c["rows_yc"][y, :, 128 * k : 128 * k + 128] = c["planar"][k, pl.ds(y + 12, 16, stride=96), :].astype(BF)
         return 0
 
-    lax.fori_loop(0, 72, gather_row, 0)
+    lax.fori_loop(0, 72, gather_row, 0, unroll=4)
 
     def column_caps(number, wp, origin, width):
         np_ = NP[number]
@@ -316,7 +344,7 @@
         m = jnp.maximum(piece[:, 0:128], piece[:, 128:256])
         return jnp.maximum(m, jnp.maximum(piece[:, 256:384], piece[:, 384:512]))
 
-    def pack(pixels, target, count, wp, lanes, row0, col0):
+    def pack(pixels, target, first, count, wp, lanes, row0, col0):
         lane = iota((wp, 128), 1)
 
         def step(i, _):
@@ -342,7 +370,7 @@
                         target[i, :, base + 128 * q : base + 128 * q + 128] = four[q].astype(BF)
             return 0
 
-        lax.fori_loop(0, count, step, 0)
+        lax.fori_loop(first, first + count, step, 0, unroll=True)
 
     def to_pixels(pieces, target, i0, wp, wr, np_):
         td = c["td"]
@@ -382,17 +410,20 @@
 
         return load
 
-    def layer(number, loads, count, g, wp, origin_y, origin_x, level, store):
+    def layer(number, loads, first, count, g, wp, origin_y, origin_x, level, store):
         height, width = 32 >> level, 256 >> level
         cap = column_caps(number, wp, origin_x, width)
 
         def step(it, _):
-            i0 = it * g
+            i0 = first + it * g
             lhs = []
             for load in loads:
                 lhs = lhs + load(i0, g)
             lhs = jnp.concatenate(lhs, axis=1) if len(lhs) > 1 else lhs[0]
-            r = nt(lhs, c["w%d" % number][...])
+            if number in FLIPPED:
+                r = jnp.dot(lhs, c["w%d" % number][...], preferred_element_type=F32)
+            else:
+                r = nt(lhs, c["w%d" % number][...])
             store(finish(number, r, cap, i0, g, wp, origin_y, height), i0)
             return 0
 
@@ -408,23 +439,45 @@
 
         return store
 
-    def windows(i, _):
-        rows = c["rows_yc"][pl.ds(2 * i, 4)].reshape(64, 1024)
-        stacked = jnp.concatenate([rows[:, 256 * s : 256 * s + 256] for s in range(4)], axis=0)
-        c["fwin"][i] = nt(c["eye"][...], stacked).astype(BF)
-        return 0
-
-    lax.fori_loop(0, 35, windows, 0)
+    def windows(first, count, g):
+        t = c["t128"]
+
+        def step(it, _):
+            i0 = first + it * g
+            for k in range(g):
+                rows = c["rows_yc"][pl.ds(2 * (i0 + k), 4)].reshape(64, 512)
+                stacked = jnp.concatenate([rows[:, 0:256], rows[:, 256:512]], axis=0)
+                turned = nt(c["eye"][...], stacked)
+                c["fwin"][i0 + k, :, 0:128] = turned.astype(BF)
+                t[k * 160 : (k + 1) * 160, :] = turned
+            for k in range(g):
+                c["fwin"][i0 + k, :, 128:256] = t[k * 160 + 1 : (k + 1) * 160 + 1, :].astype(BF)
+            return 0
+
+        if count == 1:
+            step(0, 0)
+        else:
+            lax.fori_loop(0, count, step, 0)
 
     def window_load(i0, g):
         return [c["fwin"][pl.ds(i0, g)].reshape(g * 160, 256)]
 
-    layer(0, [window_load], 7, 5, 160, -19, -35, 0, lambda p, i0: to_blocks(p, c["s1"], i0, 160, 128))
-    layer(1, [block_input(c["s1"])], 17, 2, 160, -18, -34, 0, pool_into(c["pix1"], 1, 160))
-    pack(c["pix1"], c["s2"], 17, 80, 32, 0, 8)
-    layer(2, [block_input(c["s2"])], 4, 4, 80, -8, -8, 1, pool_into(c["pix2"], 2, 80))
-    pack(c["pix2"], c["s3"], 5, 48, 64, 3, 3)
-    layer(3, [block_input(c["s3"])], 1, 4, 48, 0, 0, 2, pool_into(c["pix3o"], 3, 48))
+    def conv0(first, count, g):
+        layer(0, [window_load], first, count, g, 160, -19, -35, 0, lambda p, i0: to_blocks(p, c["s1"], i0, 160, 128))
+
+    def conv1(first, count, g):
+        layer(1, [block_input(c["s1"])], first, count, g, 160, -18, -34, 0, pool_into(c["pix1"], 1, 160))
+
+    def conv2(first, count, g):
+        layer(2, [block_input(c["s2"])], first, count, g, 80, -8, -8, 1, pool_into(c["pix2"], 2, 80))
+
+    windows(6, 2, 12)
+    conv0(6, 2, 12)
+    conv1(6, 2, 11)
+    pack(c["pix1"], c["s2"], 3, 11, 80, 32, 0, 8)
+    conv2(3, 1, 10)
+    pack(c["pix2"], c["s3"], 0, 5, 48, 64, 3, 3)
+    layer(3, [block_input(c["s3"])], 0, 1, 4, 48, 0, 0, 2, pool_into(c["pix3o"], 3, 48))
 
     lane16 = iota((16, 128), 1)
     for y in range(4):
@@ -444,35 +497,18 @@
         copy.start()
         copies.append(copy)
 
-    prepare_blocks(c["w4"], weights[4], 4, 0, 0, 64, 64)
-    prepare_blocks(c["w5"], weights[5], 5, 0, 0, 80, 128)
-    prepare_blocks(c["w6"], weights[6], 6, 0, 0, 96, 128)
-    prepare_up(c["w7"], weights[7], 7, 96, 128)
-    prepare_blocks(c["w7"], weights[7], 7, 512, 96, 64, 64)
-    prepare_blocks(c["w8"], weights[8], 8, 0, 0, 112, 128)
-    prepare_up(c["w9"], weights[9], 9, 112, 128)
-    prepare_blocks(c["w9"], weights[9], 9, 512, 112, 48, 64)
-    prepare_blocks(c["w10"], weights[10], 10, 0, 0, 96, 128)
-    prepare_blocks(c["w12"], weights[12], 12, 0, 0, 64, 64)
-    prepare_up(c["w13"], weights[13], 13, 64, 64)
-    prepare_window(c["w13"], weights[13], 13, 256, 64)
-    prepare_blocks(c["w14"], weights[14], 14, 0, 0, 64, 64)
-    c["w11"][...] = jnp.zeros(c["w11"].shape, BF)
-    prepare_up(c["w11"], weights[11], 11, 96, 128)
-    prepare_blocks(c["w11"], weights[11], 11, 512, 96, 32, 32)
-    taps = replicated_taps(weights[15], 15, 0, 32, 32)
-    c["w15f"][...] = jnp.zeros((16, 512), F32)
-    for qx in range(2):
-        for qy in range(2):
-            n = qx * 8 + qy * 3
-            for t in range(2):
-                for u in range(2):
-                    places = [tap_of(taps, 2 * t + py, 2 * u + px, qy, qx) for py in range(2) for px in range(2)]
-                    k = (t * 2 + u) * 128
-                    c["w15f"][n : n + 3, k : k + 128] = choose(places, 32, 3)
-    c["w15"][...] = c["w15f"][...].astype(BF)
-    pack(c["pix1"], c["k11"], 12, 80, 32, 5, 13)
-    pack(c["pix2"], c["k9"], 8, 48, 64, 0, 0)
+    windows(0, 1, 6)
+    windows(30, 1, 5)
+    conv0(0, 1, 6)
+    conv0(30, 1, 5)
+    conv1(0, 1, 6)
+    conv1(28, 1, 6)
+    pack(c["pix1"], c["s2"], 0, 3, 80, 32, 0, 8)
+    pack(c["pix1"], c["s2"], 14, 3, 80, 32, 0, 8)
+    conv2(0, 1, 3)
+    conv2(13, 1, 3)
+    pack(c["pix1"], c["k11"], 0, 12, 80, 32, 5, 13)
+    pack(c["pix2"], c["k9"], 0, 8, 48, 64, 0, 0)
 
     for copy in copies:
         copy.wait()
@@ -495,43 +531,43 @@
                 c["pix3"][row, pl.ds(col, 16, stride=2), :] = jnp.where(lane16 < 64, v, w)
                 c["pix3"][row, pl.ds(col + 1, 16, stride=2), :] = jnp.where(lane16 < 64, w, v)
 
-    pack(c["pix3"], c["s4"], 11, 32, 64, 3, 23)
-    pack(c["pix3"], c["k7"], 6, 32, 64, 8, 28)
-
-    layer(4, [block_input(c["s4"])], 2, 5, 32, -8, -8, 3, pool_into(c["pix4"], 4, 32))
-    pack(c["pix4"], c["s5"], 5, 16, 128, 0, 0)
-    layer(5, [block_input(c["s5"])], 1, 4, 16, -3, -3, 4, lambda p, i0: to_blocks(p, c["s6"], i0, 16, 512))
-    layer(6, [block_input(c["s6"])], 1, 3, 16, -2, -2, 4, lambda p, i0: to_pixels(p, c["r7"], i0, 16, 32, 128))
+    pack(c["pix3"], c["s4"], 0, 11, 32, 64, 3, 23)
+    pack(c["pix3"], c["k7"], 0, 6, 32, 64, 8, 28)
+
+    layer(4, [block_input(c["s4"])], 0, 1, 10, 32, -8, -8, 3, pool_into(c["pix4"], 4, 32))
+    pack(c["pix4"], c["s5"], 0, 5, 16, 128, 0, 0)
+    layer(5, [block_input(c["s5"])], 0, 1, 4, 16, -3, -3, 4, lambda p, i0: to_blocks(p, c["s6"], i0, 16, 512))
+    layer(6, [block_input(c["s6"])], 0, 1, 3, 16, -2, -2, 4, lambda p, i0: to_pixels(p, c["r7"], i0, 16, 32, 128))
     layer(
-        7, [block_input(c["r7"]), block_input(c["k7"])], 1, 5, 32, -3, -3, 3,
+        7, [block_input(c["r7"]), block_input(c["k7"])], 0, 1, 5, 32, -3, -3, 3,
         lambda p, i0: to_blocks(p, c["s8"], i0, 32, 512),
     )
-    layer(8, [block_input(c["s8"])], 1, 4, 32, -2, -2, 3, lambda p, i0: to_pixels(p, c["r9"], i0, 32, 48, 128))
+    layer(8, [block_input(c["s8"])], 0, 1, 4, 32, -2, -2, 3, lambda p, i0: to_pixels(p, c["r9"], i0, 32, 48, 128))
     layer(
-        9, [block_input(c["r9"]), block_input(c["k9"])], 1, 7, 48, -3, -3, 2,
+        9, [block_input(c["r9"]), block_input(c["k9"])], 0, 1, 7, 48, -3, -3, 2,
         lambda p, i0: to_blocks(p, c["s10"], i0, 48, 512),
     )
-    layer(10, [block_input(c["s10"])], 1, 6, 48, -2, -2, 2, lambda p, i0: to_pixels(p, c["r11"], i0, 48, 80, 128))
+    layer(10, [block_input(c["s10"])], 0, 1, 6, 48, -2, -2, 2, lambda p, i0: to_pixels(p, c["r11"], i0, 48, 80, 128))
     layer(
-        11, [block_input(c["r11"]), block_input(c["k11"])], 1, 11, 80, -3, -3, 1,
+        11, [block_input(c["r11"]), block_input(c["k11"])], 0, 1, 11, 80, -3, -3, 1,
         lambda p, i0: to_blocks(p, c["s12"], i0, 80, 256),
     )
-    layer(12, [block_input(c["s12"])], 2, 5, 80, -2, -2, 1, lambda p, i0: to_pixels(p, c["r13"], i0, 80, 144, 64))
+    layer(12, [block_input(c["s12"])], 0, 1, 10, 80, -2, -2, 1, lambda p, i0: to_pixels(p, c["r13"], i0, 80, 144, 64))
 
     def features_load(i0, g):
         return [c["fwin"][pl.ds(i0 + 8, g), 16:160, :].reshape(g * 144, 256)]
 
     layer(
-        13, [block_input(c["r13"]), features_load], 5, 4, 144, -3, -3, 0,
+        13, [block_input(c["r13"]), features_load], 0, 2, 10, 144, -3, -3, 0,
         lambda p, i0: to_blocks(p, c["s14"], i0, 144, 256),
     )
-    layer(14, [block_input(c["s14"])], 6, 3, 144, -2, -2, 0, lambda p, i0: to_blocks(p, c["s15"], i0, 144, 128))
+    layer(14, [block_input(c["s14"])], 0, 2, 9, 144, -2, -2, 0, lambda p, i0: to_blocks(p, c["s15"], i0, 144, 128))
 
     lane144 = iota((16, 144), 1)
 
     def last(i, _):
         field = jnp.concatenate([c["s15"][i], c["s15"][i + 1]], axis=1)
-        r = nt(c["w15"][...], field) + table[16:32, 0:144]
+        r = nt(c["w15"][...], field) + c["column"][...]
         r = jnp.where(lane144 < 129, r, 0.0)
         c["z0"][pl.ds(pl.multiple_of(8 * i, 8), 8), :] = r[0:8]
         c["z1"][pl.ds(pl.multiple_of(8 * i, 8), 8), :] = r[8:16]
@@ -539,7 +575,7 @@
 
     c["z0"][136:144, :] = jnp.zeros((8, 144), F32)
     c["z1"][136:144, :] = jnp.zeros((8, 144), F32)
-    lax.fori_loop(0, 17, last, 0)
+    lax.fori_loop(0, 17, last, 0, unroll=17)
     at = iota((144, 256), 1) - 2 * iota((144, 256), 0)
     even = (at == -1).astype(F32).astype(BF)
     odd = (at == 0).astype(F32).astype(BF)
@@ -555,26 +591,10 @@
             out[o, :, lanes] = c["out32"][2 * o + half].astype(BF)
 
 
-def bias_table(biases):
-    rows = []
-    offset = 0
-    for number in range(16):
-        piece = biases[offset : offset + COUT[number]]
-        offset = offset + COUT[number]
-        if number == 15:
-            six = jnp.concatenate([piece, piece, jnp.zeros((2,), F32)])
-            column = jnp.concatenate([six, six])
-            rows.append(jnp.zeros((1, 512), F32))
-            rows.append(jnp.broadcast_to(column[:, None], (16, 512)))
-        else:
-            phase = jnp.pad(piece, (0, NP[number] - COUT[number]))
-            four = jnp.concatenate([phase] * 4)
-            rows.append(jnp.pad(four, (0, 512 - 4 * NP[number]))[None])
-    return jnp.concatenate(rows, axis=0)
-
-
 def body(sizes, features, *rest):
-    weights, biases = rest[:16], rest[16]
+    weights, biases = list(rest[:16]), rest[16]
+    for number in FLIPPED:
+        weights[number] = jnp.transpose(weights[number], (0, 1, 3, 2) if number else (0, 3, 1, 2))
     vmem = pl.BlockSpec(memory_space=pltpu.VMEM)
     scratch = [pltpu.VMEM(shape, kind) for shape, kind in SCRATCH.values()]
     scratch += [pltpu.SemaphoreType.DMA((n,)) for n in (8, 8, 20, 20)]
@@ -587,7 +607,7 @@
         compiler_params=pltpu.CompilerParams(
             collective_id=0, has_side_effects=True, vmem_limit_bytes=58 << 20
         ),
-    )(features, *weights, bias_table(biases))
+    )(features, *weights, biases)
 
 
 def solution(mesh):

time: 84.9 us -> 50.3 us (0.59)
  Pallas kernels: 71.9 us -> 48.6 us
  local copies, waits for them, and re-layouts: 12.2 us -> 1.42 us
    pallas_call x1, Pallas kernels: 71.9 us -> 48.6 us  [body(): pl.pallas_call(functools.partial(kernel, sizes), out_shape=jax.ShapeDtype...]
    unnamed x24 -> x1, local copies, waits for them, and re-layouts: 7.46 us -> 1.42 us
    slice x7 -> x0, local copies, waits for them, and re-layouts: 2.64 us -> none  [bias_table(): piece = biases[offset:offset + COUT[number]]]
    concatenate x2 -> x0, local copies, waits for them, and re-layouts: 1.96 us -> none  [the longest x1 1.88 us: bias_table(): return jnp.concatenate(rows, axis=0)]
where the time goes in v2:
time: 50.3 us; the launch traced here: 50.1 us
  Pallas kernels  48.6 us (97%)
  local copies, waits for them, and re-layouts  1.42 us (3%)
    pallas_call x1, Pallas kernels, body(): pl.pallas_call(functools.partial(kernel, sizes), out_shape=jax.ShapeDtype...  48.6 us
    unnamed x1, local copies, waits for them, and re-layouts  1.42 us

profile of v2, /device:TPU:1, one launch (start us, length us, event | category | flops | bytes accessed | tf_op | source)
XLA Modules:
  0.0 50.1 jit_solution(14782954553188242497)
XLA Ops:
  0.0 48.6 %shard_map.172 = bf16[3,32,256]{2,1,0:T(8,128)(2,1)} custom-call(bf16[9,32,256]{2,1,0:T(8,128)(2,1)} %feat.1, bf16[3,9,3,32]{3,2,1,0:T(4,128)(2,1)} %bitcast.13, bf16[3,3,32,32]{3,2,1,0:T(8,128)(2,1)} %refs_1_.1, bf16[3,3,32,48]{3,2,1,0:T(8,128)(2,1)} %bitcast.12, bf16[3,3,48,64]{3,2,1,0:T(8,128)(2,1)} %bitcast.11, bf16[3,3,64,80]{3,2,1,0:T(8,128)(2,1)} %bitcast.10, ...), custom_call_target="tpu_custom_call" | custom-call | tf_op jit(solution)/shard_map/pallas_call | solution.py:601
  48.7 1.4 %copy.20 = bf16[3,32,256]{2,1,0:T(8,128)(2,1)} copy(bf16[3,32,256]{2,1,0:T(8,128)(2,1)} %shard_map.172) | data formatting | bytes 98304

commit v3 on v2

--- a/solution.py
+++ b/solution.py
@@ -15,7 +15,8 @@
 COUT = [32, 32, 48, 64, 80, 96, 96, 112, 112, 96, 96, 64, 64, 64, 32, 3]
 CIN = [9, 32, 32, 48, 64, 80, 96, 160, 112, 160, 96, 128, 64, 73, 64, 32]
 NP = [32, 32, 64, 64, 128, 128, 128, 128, 128, 128, 128, 64, 64, 64, 32, 4]
-KDIM = [256, 512, 512, 1024, 1024, 2048, 2048, 1536, 2048, 1536, 2048, 1024, 1024, 512, 1024, 512]
+KDIM = [256, 256, 512, 1024, 1024, 2048, 2048, 1536, 2048, 1536, 2048, 1024, 1024, 512, 512, 256]
+SPLIT = (1, 14, 15)
 DIRS = [(dy, dx) for dy in (-1, 0, 1) for dx in (-1, 0, 1) if (dy, dx) != (0, 0)]
 FAR = DIRS + [(dy, dx) for dy in (-3, -2, 2, 3) for dx in (-1, 0, 1)]
 
@@ -32,7 +33,7 @@
     rows_yc=((72, 16, 512), BF),
     eye=((160, 256), BF),
     fwin=((40, 160, 256), BF),
-    s1=((36, 160, 256), BF),
+    s1=((36, 160, 128), BF),
     pix1=((34, 176, 128), F32),
     s2=((17, 80, 256), BF),
     pix2=((16, 112, 128), F32),
@@ -53,8 +54,8 @@
     k11=((12, 80, 256), BF),
     s12=((11, 80, 512), BF),
     r13=((24, 144, 128), BF),
-    s14=((21, 144, 512), BF),
-    s15=((20, 144, 256), BF),
+    s14=((21, 144, 256), BF),
+    s15=((20, 144, 128), BF),
     t128=((1928, 128), F32),
     t256=((1448, 256), F32),
     t512=((360, 512), F32),
@@ -62,7 +63,7 @@
     cap128=((160, 128), F32),
     cap256=((144, 256), F32),
     cap512=((48, 512), F32),
-    w15f=((16, 512), F32),
+    w15f=((32, 256), F32),
     flat=((16, 128), F32),
     table=((16, 512), F32),
     column=((16, 144), F32),
@@ -72,7 +73,7 @@
     out32=((6, 32, 128), F32),
 )
 for _k in range(16):
-    _n = 16 if _k == 15 else 4 * NP[_k]
+    _n = 32 if _k == 15 else 256 if _k in SPLIT else 4 * NP[_k]
     SCRATCH["w%d" % _k] = ((KDIM[_k], _n) if _k in (0, 2, 3, 4, 5, 7, 9) else (_n, KDIM[_k]), BF)
 
 
@@ -109,8 +110,13 @@
             for qy in range(2):
                 for qx in range(2):
                     r, s = ky + qy, kx + qx
-                    k = offset + ((r // 2 * 2 + s // 2) * 4 + r % 2 * 2 + s % 2) * lanes
-                    put(wt, number, (qy * 2 + qx) * NP[number], k, tap)
+                    n = (qy * 2 + qx) * NP[number]
+                    if number in SPLIT:
+                        k = (r // 2 * 4 + r % 2 * 2 + s % 2) * lanes
+                        n = n + s // 2 * 128
+                    else:
+                        k = offset + ((r // 2 * 2 + s // 2) * 4 + r % 2 * 2 + s % 2) * lanes
+                    put(wt, number, n, k, tap)
 
 
 def prepare_window(wt, w, number, offset, first):
@@ -170,10 +176,15 @@
 
 def kernel(sizes, feat, *refs):
     rows_ty, cols_tx = sizes
-    weights = refs[:16]
+    sources = refs[:16]
+    weights = refs[-17:-1]
+    weight_sem = refs[-1]
+    loads = [pltpu.make_async_copy(sources[k], weights[k], weight_sem.at[k]) for k in range(16)]
+    for load in loads:
+        load.start()
     out = refs[17]
     c = dict(zip(SCRATCH, refs[18 : 18 + len(SCRATCH)]))
-    send1, recv1, send2, recv2 = refs[18 + len(SCRATCH) :]
+    send1, recv1, send2, recv2 = refs[18 + len(SCRATCH) : 22 + len(SCRATCH)]
     table = c["table"]
     ty = lax.axis_index("ty")
     tx = lax.axis_index("tx")
@@ -204,6 +215,8 @@
 
     for number in range(4):
         clear(number)
+    for load in loads[:4]:
+        load.wait()
     prepare_window(c["w0"], weights[0], 0, 0, 0)
     prepare_blocks(c["w1"], weights[1], 1, 0, 0, 32, 32)
     prepare_blocks(c["w2"], weights[2], 2, 0, 0, 32, 32)
@@ -242,6 +255,8 @@
 
     for number in range(4, 15):
         clear(number)
+    for load in loads[4:]:
+        load.wait()
     prepare_blocks(c["w4"], weights[4], 4, 0, 0, 64, 64)
     prepare_blocks(c["w5"], weights[5], 5, 0, 0, 80, 128)
     prepare_blocks(c["w6"], weights[6], 6, 0, 0, 96, 128)
@@ -257,15 +272,15 @@
     prepare_up(c["w13"], weights[13], 13, 64, 64)
     prepare_window(c["w13"], weights[13], 13, 256, 64)
     prepare_blocks(c["w14"], weights[14], 14, 0, 0, 64, 64)
-    c["w15f"][...] = jnp.zeros((16, 512), F32)
+    c["w15f"][...] = jnp.zeros((32, 256), F32)
     for ky in range(3):
         for kx in range(3):
             tap = weights[15][ky, kx].astype(F32)
             for qy in range(2):
                 for qx in range(2):
                     r, s = ky + qy, kx + qx
-                    k = ((r // 2 * 2 + s // 2) * 4 + r % 2 * 2 + s % 2) * 32
-                    n = qx * 8 + qy * 3
+                    k = (r // 2 * 4 + r % 2 * 2 + s % 2) * 32
+                    n = s // 2 * 16 + qx * 8 + qy * 3
                     c["w15f"][n : n + 3, k : k + 32] = tap
     c["w15"][...] = c["w15f"][...].astype(BF)
     for copy in copies:
@@ -314,20 +329,32 @@
         cap[0:wp, :] = jnp.where((at >= 0) & (at < width * cols_tx), BIG, 0.0)
         return cap
 
-    def finish(number, r, cap, i0, g, wp, origin, height):
+    def finish(number, r, cap, i0, g, wp, origin_y, origin_x, height, width):
         np_ = NP[number]
         n = 4 * np_
         u = jnp.maximum(r + table[number : number + 1, 0:n], 0.0)
+        low = -(origin_x // 2) if origin_x < 0 else 0
+        high = (width - origin_x) // 2
+        low, high = (low + 7) // 8 * 8, min(high // 8 * 8, wp)
         pieces = []
         for k in range(g):
-            at = origin + 2 * (i0 + k) + iota((1, n), 1) // (2 * np_) + ty * height
-            row = jnp.where((at >= 0) & (at < height * rows_ty), BIG, 0.0)
-            pieces.append(jnp.minimum(u[k * wp : (k + 1) * wp], jnp.minimum(cap[0:wp, :], row)))
+            v = u[k * wp : (k + 1) * wp]
+            parts = [jnp.minimum(v[0:low], cap[0:low, :]), v[low:high], jnp.minimum(v[high:wp], cap[high:wp, :])]
+            v = jnp.concatenate([p for p in parts if p.shape[0]], axis=0)
+            y = origin_y + 2 * (i0 + k)
+            if y < 0 or y + 2 > height:
+                at = y + iota((1, n), 1) // (2 * np_) + ty * height
+                v = jnp.minimum(v, jnp.where((at >= 0) & (at < height * rows_ty), BIG, 0.0))
+            pieces.append(v)
         return pieces
 
     def to_blocks(pieces, target, i0, wp, n):
         t = c["t%d" % n]
         g = len(pieces)
+        if target.shape[2] == n:
+            for k in range(g):
+                target[i0 + k, :, :] = pieces[k].astype(BF)
+            return
         for k in range(g):
             t[k * wp : (k + 1) * wp, :] = pieces[k]
             target[i0 + k, :, 0:n] = pieces[k].astype(BF)
@@ -424,13 +451,14 @@
                 r = jnp.dot(lhs, c["w%d" % number][...], preferred_element_type=F32)
             else:
                 r = nt(lhs, c["w%d" % number][...])
-            store(finish(number, r, cap, i0, g, wp, origin_y, height), i0)
+            if number in SPLIT:
+                c["t128"][0 : g * wp, :] = r[:, 128:256]
+                r = r[:, 0:128] + c["t128"][1 : g * wp + 1, :]
+            store(finish(number, r, cap, i0, g, wp, origin_y, origin_x, height, width), i0)
             return 0
 
-        if count == 1:
-            step(0, 0)
-        else:
-            lax.fori_loop(0, count, step, 0)
+        for it in range(count):
+            step(it, 0)
 
     def pool_into(pixels, number, wp):
         def store(pieces, i0):
@@ -479,16 +507,20 @@
     pack(c["pix2"], c["s3"], 0, 5, 48, 64, 3, 3)
     layer(3, [block_input(c["s3"])], 0, 1, 4, 48, 0, 0, 2, pool_into(c["pix3o"], 3, 48))
 
-    lane16 = iota((16, 128), 1)
-    for y in range(4):
-        even = c["pix3o"][y, pl.ds(0, 16, stride=2), :]
-        odd = c["pix3o"][y, pl.ds(1, 16, stride=2), :]
-        c["tile_out"][16 * y : 16 * y + 16, :] = jnp.where(lane16 < 64, even, odd).astype(BF)
+    lane8 = iota((8, 128), 1)
+    pieces = []
+    for half in range(2):
+        for y in range(4):
+            even = c["pix3o"][y, pl.ds(16 * half, 8, stride=2), :]
+            odd = c["pix3o"][y, pl.ds(16 * half + 1, 8, stride=2), :]
+            pieces.append(jnp.where(lane8 < 64, even, odd))
+    c["tile_out"][...] = jnp.concatenate(pieces, axis=0).astype(BF)
     copies = []
     for number, (dy, dx) in enumerate(FAR):
+        rows = pl.ds(0, 64) if dx == 0 else pl.ds(32, 32) if dx == 1 else pl.ds(0, 32)
         copy = pltpu.make_async_remote_copy(
-            src_ref=c["tile_out"],
-            dst_ref=c["tiles_in"].at[number],
+            src_ref=c["tile_out"].at[rows],
+            dst_ref=c["tiles_in"].at[number, rows],
             send_sem=send2.at[number],
             recv_sem=recv2.at[number],
             device_id=device(dy, dx),
@@ -521,15 +553,17 @@
             else:
                 ok = (ty + ky >= 0) & (ty + ky < rows_ty) & (tx + kx >= 0) & (tx + kx < cols_tx)
                 tile = jnp.where(jnp.where(ok, 1.0, 0.0) > 0, c["tiles_in"][slot[-ky, -kx]].astype(F32), 0.0)
+            halves = (0, 1) if kx == 0 else (1,) if kx == -1 else (0,)
             for y in range(4):
                 if ky == -3 and y < 3 or ky == 3 and y > 0:
                     continue
-                v = tile[16 * y : 16 * y + 16]
-                w = pltpu.roll(v, 64, 1)
-                row = 12 + 4 * ky + y
-                col = 32 * (kx + 1)
-                c["pix3"][row, pl.ds(col, 16, stride=2), :] = jnp.where(lane16 < 64, v, w)
-                c["pix3"][row, pl.ds(col + 1, 16, stride=2), :] = jnp.where(lane16 < 64, w, v)
+                for half in halves:
+                    v = tile[32 * half + 8 * y : 32 * half + 8 * y + 8]
+                    w = pltpu.roll(v, 64, 1)
+                    row = 12 + 4 * ky + y
+                    col = 32 * (kx + 1) + 16 * half
+                    c["pix3"][row, pl.ds(col, 8, stride=2), :] = jnp.where(lane8 < 64, v, w)
+                    c["pix3"][row, pl.ds(col + 1, 8, stride=2), :] = jnp.where(lane8 < 64, w, v)
 
     pack(c["pix3"], c["s4"], 0, 11, 32, 64, 3, 23)
     pack(c["pix3"], c["k7"], 0, 6, 32, 64, 8, 28)
@@ -558,7 +592,11 @@
         return [c["fwin"][pl.ds(i0 + 8, g), 16:160, :].reshape(g * 144, 256)]
 
     layer(
-        13, [block_input(c["r13"]), features_load], 0, 2, 10, 144, -3, -3, 0,
+        13, [block_input(c["r13"]), features_load], 0, 1, 10, 144, -3, -3, 0,
+        lambda p, i0: to_blocks(p, c["s14"], i0, 144, 256),
+    )
+    layer(
+        13, [block_input(c["r13"]), features_load], 10, 1, 9, 144, -3, -3, 0,
         lambda p, i0: to_blocks(p, c["s14"], i0, 144, 256),
     )
     layer(14, [block_input(c["s14"])], 0, 2, 9, 144, -2, -2, 0, lambda p, i0: to_blocks(p, c["s15"], i0, 144, 128))
@@ -567,7 +605,8 @@
 
     def last(i, _):
         field = jnp.concatenate([c["s15"][i], c["s15"][i + 1]], axis=1)
-        r = nt(c["w15"][...], field) + c["column"][...]
+        r = nt(c["w15"][...], field)
+        r = r[0:16] + pltpu.roll(r[16:32], 143, 1) + c["column"][...]
         r = jnp.where(lane144 < 129, r, 0.0)
         c["z0"][pl.ds(pl.multiple_of(8 * i, 8), 8), :] = r[0:8]
         c["z1"][pl.ds(pl.multiple_of(8 * i, 8), 8), :] = r[8:16]
@@ -598,10 +637,11 @@
     vmem = pl.BlockSpec(memory_space=pltpu.VMEM)
     scratch = [pltpu.VMEM(shape, kind) for shape, kind in SCRATCH.values()]
     scratch += [pltpu.SemaphoreType.DMA((n,)) for n in (8, 8, 20, 20)]
+    scratch += [pltpu.VMEM(w.shape, BF) for w in weights] + [pltpu.SemaphoreType.DMA((16,))]
     return pl.pallas_call(
         functools.partial(kernel, sizes),
         out_shape=jax.ShapeDtypeStruct((3, 32, 256), BF),
-        in_specs=[vmem] * 18,
+        in_specs=[vmem] + [pl.BlockSpec(memory_space=pl.ANY)] * 16 + [vmem],
         out_specs=vmem,
         scratch_shapes=scratch,
         compiler_params=pltpu.CompilerParams(

time: 50.3 us -> 45.7 us (0.909)
  Pallas kernels: 48.6 us -> 44.1 us
    pallas_call x1, Pallas kernels: 48.6 us -> 44.1 us  [body(): pl.pallas_call(functools.partial(kernel, sizes), out_shape=jax.ShapeDtype...]
where the time goes in v3:
time: 45.7 us; the launch traced here: 45.5 us
  Pallas kernels  44.1 us (96%)
  local copies, waits for them, and re-layouts  1.42 us (3%)
    pallas_call x1, Pallas kernels, body(): pl.pallas_call(functools.partial(kernel, sizes), out_shape=jax.ShapeDtype...  44.1 us
    unnamed x1, local copies, waits for them, and re-layouts  1.42 us

profile of v3, /device:TPU:1, one launch (start us, length us, event | category | flops | bytes accessed | tf_op | source)
XLA Modules:
  0.0 45.5 jit_solution(8191337547338370090)
XLA Ops:
  0.0 44.1 %shard_map.172 = bf16[3,32,256]{2,1,0:T(8,128)(2,1)} custom-call(bf16[9,32,256]{2,1,0:T(8,128)(2,1)} %feat.1, bf16[3,9,3,32]{3,2,1,0:T(4,128)(2,1)} %bitcast.13, bf16[3,3,32,32]{3,2,1,0:T(8,128)(2,1)} %refs_1_.1, bf16[3,3,32,48]{3,2,1,0:T(8,128)(2,1)} %bitcast.12, bf16[3,3,48,64]{3,2,1,0:T(8,128)(2,1)} %bitcast.11, bf16[3,3,64,80]{3,2,1,0:T(8,128)(2,1)} %bitcast.10, ...), custom_call_target="tpu_custom_call" | custom-call | tf_op jit(solution)/shard_map/pallas_call | solution.py:641
  44.1 1.4 %copy.20 = bf16[3,32,256]{2,1,0:T(8,128)(2,1)} copy(bf16[3,32,256]{2,1,0:T(8,128)(2,1)} %shard_map.172) | data formatting | bytes 98304

commit v4 on v3

--- a/solution.py
+++ b/solution.py
@@ -60,9 +60,6 @@
     t256=((1448, 256), F32),
     t512=((360, 512), F32),
     td=((20, 184, 128), F32),
-    cap128=((160, 128), F32),
-    cap256=((144, 256), F32),
-    cap512=((48, 512), F32),
     w15f=((32, 256), F32),
     flat=((16, 128), F32),
     table=((16, 512), F32),
@@ -190,11 +187,34 @@
     tx = lax.axis_index("tx")
 
     def device(dy, dx):
-        return (lax.rem(ty + dy + rows_ty, rows_ty), lax.rem(tx + dx + cols_tx, cols_tx))
+        return (ty + dy, tx + dx)
+
+    def exists(dy, dx):
+        found = None
+        for here, step, size in ((ty, dy, rows_ty), (tx, dx, cols_tx)):
+            if step:
+                inside = here + step < size if step > 0 else here + step >= 0
+                found = inside if found is None else found & inside
+        return found
+
+    def exchange(copies):
+        for dy, dx, copy in copies:
+            pl.when(exists(dy, dx))(copy.start)
+
+        def wait():
+            for dy, dx, copy in copies:
+                pl.when(exists(dy, dx))(copy.wait_send)
+                pl.when(exists(-dy, -dx))(copy.wait_recv)
+
+        return wait
 
     barrier = pltpu.get_barrier_semaphore()
     for dy, dx in FAR:
-        pl.semaphore_signal(barrier, inc=1, device_id=device(dy, dx), device_id_type=MESH)
+
+        @pl.when(exists(dy, dx))
+        def greet(dy=dy, dx=dx):
+            pl.semaphore_signal(barrier, inc=1, device_id=device(dy, dx), device_id_type=MESH)
+
 
     lane9 = iota((9, 8, 128), 2)
     for side in range(2):
@@ -234,7 +254,13 @@
     for k in range(4):
         c["planar"][k, 864:1536, :] = jnp.zeros((672, 128), F32)
 
-    pl.semaphore_wait(barrier, len(FAR))
+    def reach(here, size, most):
+        total = 1
+        for k in range(1, most + 1):
+            total = total + lax.div(here + size - k, size) + 1 - lax.div(here + k, size)
+        return total
+
+    pl.semaphore_wait(barrier, reach(ty, rows_ty, 3) * reach(tx, cols_tx, 1) - 1)
     copies = []
     for number, (dy, dx) in enumerate(DIRS):
         if dx == 0:
@@ -250,8 +276,9 @@
             device_id=device(dy, dx),
             device_id_type=MESH,
         )
-        copy.start()
-        copies.append(copy)
+        copies.append((dy, dx, copy))
+
+    wait = exchange(copies)
 
     for number in range(4, 15):
         clear(number)
@@ -283,8 +310,7 @@
                     n = s // 2 * 16 + qx * 8 + qy * 3
                     c["w15f"][n : n + 3, k : k + 32] = tap
     c["w15"][...] = c["w15f"][...].astype(BF)
-    for copy in copies:
-        copy.wait()
+    wait()
 
     first_row = jnp.where(ty > 0, 1.0, 0.0)
     last_row = jnp.where(ty < rows_ty - 1, 1.0, 0.0)
@@ -321,26 +347,28 @@
 
     lax.fori_loop(0, 72, gather_row, 0, unroll=4)
 
-    def column_caps(number, wp, origin, width):
+    def column_cap(number, first, count, origin, width):
         np_ = NP[number]
         n = 4 * np_
-        cap = c["cap%d" % n]
-        at = origin + 2 * iota((wp, n), 0) + (iota((wp, n), 1) // np_) % 2 + tx * width
-        cap[0:wp, :] = jnp.where((at >= 0) & (at < width * cols_tx), BIG, 0.0)
-        return cap
-
-    def finish(number, r, cap, i0, g, wp, origin_y, origin_x, height, width):
+        at = origin + 2 * (first + iota((count, n), 0)) + (iota((count, n), 1) // np_) % 2 + tx * width
+        return jnp.where((at >= 0) & (at < width * cols_tx), BIG, 0.0)
+
+    def edges(wp, origin, width):
+        low = (-(origin // 2) + 7) // 8 * 8
+        return low, min((width - origin) // 2 // 8 * 8, wp)
+
+    def finish(number, r, caps, i0, g, wp, origin_y, origin_x, height, width):
         np_ = NP[number]
         n = 4 * np_
         u = jnp.maximum(r + table[number : number + 1, 0:n], 0.0)
-        low = -(origin_x // 2) if origin_x < 0 else 0
-        high = (width - origin_x) // 2
-        low, high = (low + 7) // 8 * 8, min(high // 8 * 8, wp)
+        low, high = edges(wp, origin_x, width)
         pieces = []
         for k in range(g):
             v = u[k * wp : (k + 1) * wp]
-            parts = [jnp.minimum(v[0:low], cap[0:low, :]), v[low:high], jnp.minimum(v[high:wp], cap[high:wp, :])]
-            v = jnp.concatenate([p for p in parts if p.shape[0]], axis=0)
+            parts = [jnp.minimum(v[0:low], caps[0])] if low else []
+            parts = parts + ([v[low:high]] if high > low else [])
+            parts = parts + ([jnp.minimum(v[high:wp], caps[1])] if wp > high else [])
+            v = jnp.concatenate(parts, axis=0) if len(parts) > 1 else parts[0]
             y = origin_y + 2 * (i0 + k)
             if y < 0 or y + 2 > height:
                 at = y + iota((1, n), 1) // (2 * np_) + ty * height
@@ -439,7 +467,11 @@
 
     def layer(number, loads, first, count, g, wp, origin_y, origin_x, level, store):
         height, width = 32 >> level, 256 >> level
-        cap = column_caps(number, wp, origin_x, width)
+        low, high = edges(wp, origin_x, width)
+        caps = (
+            column_cap(number, 0, low, origin_x, width) if low else None,
+            column_cap(number, high, wp - high, origin_x, width) if wp > high else None,
+        )
 
         def step(it, _):
             i0 = first + it * g
@@ -454,7 +486,7 @@
             if number in SPLIT:
                 c["t128"][0 : g * wp, :] = r[:, 128:256]
                 r = r[:, 0:128] + c["t128"][1 : g * wp + 1, :]
-            store(finish(number, r, cap, i0, g, wp, origin_y, origin_x, height, width), i0)
+            store(finish(number, r, caps, i0, g, wp, origin_y, origin_x, height, width), i0)
             return 0
 
         for it in range(count):
@@ -526,8 +558,9 @@
             device_id=device(dy, dx),
             device_id_type=MESH,
         )
-        copy.start()
-        copies.append(copy)
+        copies.append((dy, dx, copy))
+
+    wait = exchange(copies)
 
     windows(0, 1, 6)
     windows(30, 1, 5)
@@ -542,8 +575,7 @@
     pack(c["pix1"], c["k11"], 0, 12, 80, 32, 5, 13)
     pack(c["pix2"], c["k9"], 0, 8, 48, 64, 0, 0)
 
-    for copy in copies:
-        copy.wait()
+    wait()
 
     slot = {d: n for n, d in enumerate(FAR)}
     for ky in range(-3, 4):

time: 45.7 us -> 36.2 us (0.79)
  Pallas kernels: 44.1 us -> 34.6 us
    pallas_call x1, Pallas kernels: 44.1 us -> 34.6 us  [body(): pl.pallas_call(functools.partial(kernel, sizes), out_shape=jax.ShapeDtype...]
where the time goes in v4:
time: 36.2 us; the launch traced here: 36 us
  Pallas kernels  34.6 us (96%)
  local copies, waits for them, and re-layouts  1.42 us (4%)
    pallas_call x1, Pallas kernels, body(): pl.pallas_call(functools.partial(kernel, sizes), out_shape=jax.ShapeDtype...  34.6 us
    unnamed x1, local copies, waits for them, and re-layouts  1.42 us

profile of v4, /device:TPU:1, one launch (start us, length us, event | category | flops | bytes accessed | tf_op | source)
XLA Modules:
  0.0 36.0 jit_solution(854030033796022780)
XLA Ops:
  0.0 34.6 %shard_map.172 = bf16[3,32,256]{2,1,0:T(8,128)(2,1)} custom-call(bf16[9,32,256]{2,1,0:T(8,128)(2,1)} %feat.1, bf16[3,9,3,32]{3,2,1,0:T(4,128)(2,1)} %bitcast.13, bf16[3,3,32,32]{3,2,1,0:T(8,128)(2,1)} %refs_1_.1, bf16[3,3,32,48]{3,2,1,0:T(8,128)(2,1)} %bitcast.12, bf16[3,3,48,64]{3,2,1,0:T(8,128)(2,1)} %bitcast.11, bf16[3,3,64,80]{3,2,1,0:T(8,128)(2,1)} %bitcast.10, ...), custom_call_target="tpu_custom_call" | custom-call | tf_op jit(solution)/shard_map/pallas_call | solution.py:673
  34.6 1.4 %copy.20 = bf16[3,32,256]{2,1,0:T(8,128)(2,1)} copy(bf16[3,32,256]{2,1,0:T(8,128)(2,1)} %shard_map.172) | data formatting | bytes 98304

commit v5 on v4

--- a/solution.py
+++ b/solution.py
@@ -177,8 +177,6 @@
     weights = refs[-17:-1]
     weight_sem = refs[-1]
     loads = [pltpu.make_async_copy(sources[k], weights[k], weight_sem.at[k]) for k in range(16)]
-    for load in loads:
-        load.start()
     out = refs[17]
     c = dict(zip(SCRATCH, refs[18 : 18 + len(SCRATCH)]))
     send1, recv1, send2, recv2 = refs[18 + len(SCRATCH) : 22 + len(SCRATCH)]
@@ -198,7 +196,7 @@
         return found
 
     def exchange(copies):
-        for dy, dx, copy in copies:
+        for dy, dx, copy in sorted(copies, key=lambda c: c[1] == 0):
             pl.when(exists(dy, dx))(copy.start)
 
         def wait():
@@ -209,12 +207,15 @@
         return wait
 
     barrier = pltpu.get_barrier_semaphore()
-    for dy, dx in FAR:
+    for dy, dx in sorted(FAR, key=lambda d: d[1] == 0):
 
         @pl.when(exists(dy, dx))
         def greet(dy=dy, dx=dx):
             pl.semaphore_signal(barrier, inc=1, device_id=device(dy, dx), device_id_type=MESH)
 
+
+    for load in loads:
+        load.start()
 
     lane9 = iota((9, 8, 128), 2)
     for side in range(2):
@@ -338,14 +339,14 @@
             c["planar"][k, pl.ds(pl.multiple_of(ch * 96, 96), 96), :] = wide[:, 128 * k : 128 * k + 128]
         return 0
 
-    lax.fori_loop(0, 9, spread_channel, 0, unroll=3)
+    lax.fori_loop(0, 9, spread_channel, 0, unroll=9)
 
     def gather_row(y, _):
         for k in range(4):
             c["rows_yc"][y, :, 128 * k : 128 * k + 128] = c["planar"][k, pl.ds(y + 12, 16, stride=96), :].astype(BF)
         return 0
 
-    lax.fori_loop(0, 72, gather_row, 0, unroll=4)
+    lax.fori_loop(0, 72, gather_row, 0, unroll=24)
 
     def column_cap(number, first, count, origin, width):
         np_ = NP[number]
@@ -514,10 +515,8 @@
                 c["fwin"][i0 + k, :, 128:256] = t[k * 160 + 1 : (k + 1) * 160 + 1, :].astype(BF)
             return 0
 
-        if count == 1:
-            step(0, 0)
-        else:
-            lax.fori_loop(0, count, step, 0)
+        for it in range(count):
+            step(it, 0)
 
     def window_load(i0, g):
         return [c["fwin"][pl.ds(i0, g)].reshape(g * 160, 256)]

time: 36.2 us -> 35 us (0.967)
  Pallas kernels: 34.6 us -> 33.4 us
    pallas_call x1, Pallas kernels: 34.6 us -> 33.4 us  [body(): pl.pallas_call(functools.partial(kernel, sizes), out_shape=jax.ShapeDtype...]
where the time goes in v5:
time: 35 us; the launch traced here: 34.8 us
  Pallas kernels  33.4 us (95%)
  local copies, waits for them, and re-layouts  1.42 us (4%)
    pallas_call x1, Pallas kernels, body(): pl.pallas_call(functools.partial(kernel, sizes), out_shape=jax.ShapeDtype...  33.4 us
    unnamed x1, local copies, waits for them, and re-layouts  1.42 us

profile of v5, /device:TPU:1, one launch (start us, length us, event | category | flops | bytes accessed | tf_op | source)
XLA Modules:
  0.0 34.8 jit_solution(15559461176857952721)
XLA Ops:
  0.0 33.4 %shard_map.172 = bf16[3,32,256]{2,1,0:T(8,128)(2,1)} custom-call(bf16[9,32,256]{2,1,0:T(8,128)(2,1)} %feat.1, bf16[3,9,3,32]{3,2,1,0:T(4,128)(2,1)} %bitcast.13, bf16[3,3,32,32]{3,2,1,0:T(8,128)(2,1)} %refs_1_.1, bf16[3,3,32,48]{3,2,1,0:T(8,128)(2,1)} %bitcast.12, bf16[3,3,48,64]{3,2,1,0:T(8,128)(2,1)} %bitcast.11, bf16[3,3,64,80]{3,2,1,0:T(8,128)(2,1)} %bitcast.10, ...), custom_call_target="tpu_custom_call" | custom-call | tf_op jit(solution)/shard_map/pallas_call | solution.py:672
  33.4 1.4 %copy.20 = bf16[3,32,256]{2,1,0:T(8,128)(2,1)} copy(bf16[3,32,256]{2,1,0:T(8,128)(2,1)} %shard_map.172) | data formatting | bytes 98304

commit v6 on v5

--- a/solution.py
+++ b/solution.py
@@ -346,7 +346,7 @@
             c["rows_yc"][y, :, 128 * k : 128 * k + 128] = c["planar"][k, pl.ds(y + 12, 16, stride=96), :].astype(BF)
         return 0
 
-    lax.fori_loop(0, 72, gather_row, 0, unroll=24)
+    lax.fori_loop(0, 72, gather_row, 0, unroll=72)
 
     def column_cap(number, first, count, origin, width):
         np_ = NP[number]

time: 35 us -> 34.8 us (level)
  no operation moved by 1% of the time
where the time goes in v6:
time: 34.8 us; the launch traced here: 34.6 us
  Pallas kernels  33.1 us (95%)
  local copies, waits for them, and re-layouts  1.42 us (4%)
    pallas_call x1, Pallas kernels, body(): pl.pallas_call(functools.partial(kernel, sizes), out_shape=jax.ShapeDtype...  33.1 us
    unnamed x1, local copies, waits for them, and re-layouts  1.42 us

profile of v6, /device:TPU:1, one launch (start us, length us, event | category | flops | bytes accessed | tf_op | source)
XLA Modules:
  0.0 34.6 jit_solution(14627353140222242267)
XLA Ops:
  0.0 33.1 %shard_map.172 = bf16[3,32,256]{2,1,0:T(8,128)(2,1)} custom-call(bf16[9,32,256]{2,1,0:T(8,128)(2,1)} %feat.1, bf16[3,9,3,32]{3,2,1,0:T(4,128)(2,1)} %bitcast.13, bf16[3,3,32,32]{3,2,1,0:T(8,128)(2,1)} %refs_1_.1, bf16[3,3,32,48]{3,2,1,0:T(8,128)(2,1)} %bitcast.12, bf16[3,3,48,64]{3,2,1,0:T(8,128)(2,1)} %bitcast.11, bf16[3,3,64,80]{3,2,1,0:T(8,128)(2,1)} %bitcast.10, ...), custom_call_target="tpu_custom_call" | custom-call | tf_op jit(solution)/shard_map/pallas_call | solution.py:672
  33.2 1.4 %copy.20 = bf16[3,32,256]{2,1,0:T(8,128)(2,1)} copy(bf16[3,32,256]{2,1,0:T(8,128)(2,1)} %shard_map.172) | data formatting | bytes 98304
